TPU v7x, 768 devices: a whole 4x8x12 slice. The times are simulated.
768 devices in a mesh: yy: 2 (over core), lat: 24 (over x_lo, z), lon: 16 (over x_hi, y).
Axes of the slice: x: 4 (x_hi: 2, x_lo: 2; x = x_hi * 2 + x_lo), y: 8, z: 12, core: 2. Of those that a mesh axis runs over, the one named last changes fastest.
Arguments:
- fields_in: float32 [2, 5, 384, 36864], P('yy', None, 'lat', 'lon'), may hold values from -6 to 6
- viscosity: float32 [2, 384, 36864], P('yy', 'lat', 'lon'), may hold values from 0.02 to 0.4
- lat_weights: float32 [2, 24, 16, 18, 128], P('yy', 'lat', 'lon'), may hold values from -0.5 to 0.5
- lon_weights: float32 [2, 24, 16, 6, 128], P('yy', 'lat', 'lon'), may hold values from -0.5 to 0.5
- lat_angles: float32 [2, 24, 16, 18], P('yy', 'lat', 'lon'), may hold values from -3.140625 to 3.140625
- lon_angles: float32 [2, 24, 16, 6], P('yy', 'lat', 'lon'), may hold values from -3.140625 to 3.140625
- patch_rows: int32 [2, 24, 16, 2], P('yy', 'lat', 'lon'), may hold values from 0 to 8
- patch_cols: int32 [2, 24, 16, 2], P('yy', 'lat', 'lon'), may hold values from 0 to 56
- lat_pairing: int32 [2, 16, 24], P(None, 'lon'), may hold values from 0 to 23, each once within a row
- lon_pairing: int32 [2, 24, 16], P(None, 'lat'), may hold values from 0 to 15, each once within a row
Outputs:
- fields_out: float32 [2, 5, 384, 36864], P('yy', None, 'lat', 'lon')
Inputs may be any that keep to these rules, and one draw needn't show every extreme that they name: `lat_pairing`: for every receiving panel and longitude tile, the entries over the 24 source tiles are each block number once. `lon_pairing`: for every receiving panel and latitude tile, the entries over the 16 source tiles are each block number once.
All inputs are finite; a program needn't handle non-finite values.
Results may differ from a plain program's by a relative error of at most 0.0003.
Values sent between devices are 32-bit elements; how exact they have to be, the bound alone decides.
A program may use at most 32 MiB of HBM per device.

v0:
```python
import math

import jax
import jax.numpy as jnp
from jax import lax
from jax.sharding import PartitionSpec as P

FIELDS = 5
LEV = 32
PATCH_H = 8
PATCH_W = 16


TIME_STEP = 0.2
KAPPA_PRESS = 0.4
GAMMA_HEAT = 1.4


def extended(block, sides, width):
    for axis, dim in sides:
        count = lax.axis_size(axis)
        forward = [(i, i + 1) for i in range(count - 1)]
        backward = [(target, source) for source, target in forward]
        low = lax.ppermute(
            lax.slice_in_dim(block, block.shape[dim] - width, None, axis=dim), axis, forward
        )
        high = lax.ppermute(lax.slice_in_dim(block, 0, width, axis=dim), axis, backward)
        block = jnp.concatenate([low, block, high], axis=dim)
    return block


def row_shift(padded, offset):
    height = padded.shape[1] - 6
    width = padded.shape[2] - 6 * LEV
    return padded[:, 3 + offset : 3 + offset + height, 3 * LEV : 3 * LEV + width]


def col_shift(padded, offset):
    height = padded.shape[1] - 6
    width = padded.shape[2] - 6 * LEV
    begin = (3 + offset) * LEV
    return padded[:, 3 : 3 + height, begin : begin + width]


def sixth_order(padded, shifter):
    return (
        45.0 * (shifter(padded, 1) - shifter(padded, -1))
        - 9.0 * (shifter(padded, 2) - shifter(padded, -2))
        + (shifter(padded, 3) - shifter(padded, -3))
    ) / 60.0


def vertical(interior):
    widened = jnp.pad(interior, ((0, 0), (0, 0), (1, 1)))
    level = jnp.arange(interior.shape[2], dtype=jnp.int32) % LEV
    upper = jnp.where((level == LEV - 1)[None, None, :], 0.0, widened[..., 2:])
    lower = jnp.where((level == 0)[None, None, :], 0.0, widened[..., :-2])
    return 0.5 * (upper - lower)


def latitude_cosine(first_row, count, total_rows):
    rows_float = (first_row + jnp.arange(count, dtype=jnp.int32)).astype(jnp.float32)
    return jnp.cos((rows_float + 0.5 - 0.5 * total_rows) * (0.5 * math.pi / total_rows))


def tendency(padded, cell_visc, cosine):
    interior = row_shift(padded, 0)
    metric = cosine[None, :, None]
    along_lat = sixth_order(padded, row_shift)
    along_lon = sixth_order(padded, col_shift) / metric
    along_lev = vertical(interior)
    laplace = (
        row_shift(padded, 1)
        + row_shift(padded, -1)
        - 2.0 * interior
        + (col_shift(padded, 1) + col_shift(padded, -1) - 2.0 * interior) / (metric * metric)
    )
    advection = interior[1:2] * along_lon + interior[2:3] * along_lat + interior[3:4] * along_lev
    divergence = along_lon[1] + along_lat[2] + along_lev[3]
    forcing = jnp.stack(
        [
            -divergence,
            -KAPPA_PRESS * along_lon[4],
            -KAPPA_PRESS * along_lat[4],
            -KAPPA_PRESS * along_lev[4] - interior[0],
            -GAMMA_HEAT * divergence,
        ]
    )
    return forcing - advection + cell_visc[None] * laplace


def rim_export(merged_fields, row_start, col_start, matrix, angles):
    tile_fields = merged_fields.reshape(
        merged_fields.shape[0], merged_fields.shape[1], merged_fields.shape[2] // LEV, LEV
    )
    zero_index = jnp.zeros((), jnp.int32)
    source_patch = lax.dynamic_slice(
        tile_fields,
        (zero_index, row_start, col_start, zero_index),
        (tile_fields.shape[0], PATCH_H, PATCH_W, LEV),
    )
    flat = source_patch.reshape(tile_fields.shape[0], PATCH_H * PATCH_W, LEV)
    interp = jnp.einsum("ts,fsl->ftl", matrix, flat, precision=lax.Precision.HIGHEST)
    cos_angle = jnp.cos(angles)[:, None]
    sin_angle = jnp.sin(angles)[:, None]
    east_part = cos_angle * interp[1] + sin_angle * interp[2]
    north_part = -sin_angle * interp[1] + cos_angle * interp[2]
    return jnp.stack([interp[0], east_part, north_part, interp[3], interp[4]])


def place_blocks(pairing_row, count, panel, pieces):
    rows_here = pieces.shape[0]
    sources = jnp.arange(rows_here, dtype=jnp.int32)
    positions = jnp.arange(count, dtype=jnp.int32)
    usable = sources // count != panel
    sources = sources % count
    block_of = jnp.sum(
        jnp.where(sources[:, None] == positions[None, :], pairing_row[None, :], 0), axis=1
    )
    selector = jnp.logical_and(block_of[:, None] == positions[None, :], usable[:, None]).astype(
        jnp.float32
    )
    return jnp.einsum("mk,mftl->fktl", selector, pieces, precision=lax.Precision.HIGHEST)


def on_device(
    fields_in,
    viscosity,
    lat_weights,
    lon_weights,
    lat_angles,
    lon_angles,
    patch_rows,
    patch_cols,
    lat_pairing,
    lon_pairing,
):
    panel = lax.axis_index("yy")
    lat_index = lax.axis_index("lat")
    lon_index = lax.axis_index("lon")
    lat_count = lax.axis_size("lat")
    lon_count = lax.axis_size("lon")
    start_fields = fields_in[0]
    tile_rows = start_fields.shape[1]
    merged_width = start_fields.shape[2]
    edge_width = 3 * LEV
    cosine = latitude_cosine(lat_index * tile_rows, tile_rows, tile_rows * lat_count)
    lat_row = lax.dynamic_index_in_dim(lat_pairing[:, 0, :], panel, 0, keepdims=False)
    lon_row = lax.dynamic_index_in_dim(lon_pairing[:, 0, :], panel, 0, keepdims=False)
    cell_visc = viscosity[0]

    def section_rate(current):
        lat_part = rim_export(
            current,
            patch_rows[0, 0, 0, 0],
            patch_cols[0, 0, 0, 0],
            lat_weights[0, 0, 0],
            lat_angles[0, 0, 0],
        )
        lon_part = rim_export(
            current,
            patch_rows[0, 0, 0, 1],
            patch_cols[0, 0, 0, 1],
            lon_weights[0, 0, 0],
            lon_angles[0, 0, 0],
        )
        lat_total = place_blocks(
            lat_row,
            lat_count,
            panel,
            lax.all_gather(lat_part[None], ("yy", "lat"), axis=0, tiled=True),
        )
        lon_total = place_blocks(
            lon_row,
            lon_count,
            panel,
            lax.all_gather(lon_part[None], ("yy", "lon"), axis=0, tiled=True),
        )
        lat_edges = lat_total.reshape(FIELDS, 6, merged_width)
        west_edges = lon_total[:, :, 0:3].reshape(FIELDS, tile_rows, edge_width)
        east_edges = lon_total[:, :, 3:6].reshape(FIELDS, tile_rows, edge_width)
        widened = extended(current, (("lon", 2),), edge_width)
        padded = extended(widened, (("lat", 1),), 3)
        ghost_south = jnp.where(
            lat_index == 0,
            lat_edges[:, 0:3],
            padded[:, 0:3, edge_width : edge_width + merged_width],
        )
        padded = padded.at[:, 0:3, edge_width : edge_width + merged_width].set(ghost_south)
        ghost_north = jnp.where(
            lat_index == lat_count - 1,
            lat_edges[:, 3:6],
            padded[:, tile_rows + 3 : tile_rows + 6, edge_width : edge_width + merged_width],
        )
        padded = padded.at[
            :, tile_rows + 3 : tile_rows + 6, edge_width : edge_width + merged_width
        ].set(ghost_north)
        ghost_west = jnp.where(
            lon_index == 0, west_edges, padded[:, 3 : 3 + tile_rows, 0:edge_width]
        )
        padded = padded.at[:, 3 : 3 + tile_rows, 0:edge_width].set(ghost_west)
        east_start = edge_width + merged_width
        ghost_east = jnp.where(
            lon_index == lon_count - 1,
            east_edges,
            padded[:, 3 : 3 + tile_rows, east_start : east_start + edge_width],
        )
        padded = padded.at[:, 3 : 3 + tile_rows, east_start : east_start + edge_width].set(
            ghost_east
        )
        return tendency(padded, cell_visc, cosine)

    first_section = start_fields + TIME_STEP * section_rate(start_fields)
    second_rate = section_rate(first_section)
    result = 0.5 * (start_fields + first_section + TIME_STEP * second_rate)
    return result[None]


def solution(mesh):
    in_specs = (
        P("yy", None, "lat", "lon"),
        P("yy", "lat", "lon"),
        P("yy", "lat", "lon", None, None),
        P("yy", "lat", "lon", None, None),
        P("yy", "lat", "lon", None),
        P("yy", "lat", "lon", None),
        P("yy", "lat", "lon", None),
        P("yy", "lat", "lon", None),
        P(None, "lon", None),
        P(None, "lat", None),
    )
    out_specs = P("yy", None, "lat", "lon")
    return jax.shard_map(
        on_device, mesh=mesh, in_specs=in_specs, out_specs=out_specs, check_vma=False
    )
```

profile of v0, /device:TPU:6, one launch (start us, length us, event | category | flops | bytes accessed | tf_op | source)
XLA Modules:
  0.0 503.5 jit_solution(12308265038389141977)
XLA Ops:
  0.0 0.9 fusion.87
  0.9 6.2 %collective-permute-start.1 = (f32[5,16,96]{2,1,0:T(8,128)S(1)}, f32[5,16,96]{2,1,0:T(8,128)S(1)}, u32[]{:S(2)}, u32[]{:S(2)}) collective-permute-start(f32[5,16,96]{2,1,0:T(8,128)S(1)} %get-tuple-element.131), channel_id=1, source_target_pairs={{1,0},{2,1},{3,2},{4,3},{5,4},{6,5},{7,6},{8,7},{9,8},{10,9},{11,1... | collective-permute-start | bytes 92168 | tf_op jit(solution)/shard_map/ppermute | solution.py:27
  7.1 1.9 collective-permute-start
  9.1 1.3 fusion.91
  12.8 1.3 fusion.90
  16.5 0.7 fusion.79
  17.2 0.7 sine_bitcast_fusion.1
  17.9 0.7 fusion.80
  18.7 0.7 sine_bitcast_fusion
  19.4 3.1 reshape_squeeze.4
  25.0 1.3 constant_dynamic-slice_fusion.3
  26.6 0.3 convolution_bitcast_fusion.3
  27.0 79.5 %all-gather.1 = f32[160,6,32]{2,1,0:T(8,128)S(1)} all-gather(f32[5,6,32]{2,1,0:T(8,128)S(1)} %pad_maximum_fusion.4), channel_id=3, replica_groups=mesh['yy'=2,'lat'=24,'lon'=16] {'yy','lon'}, dimensions={0}, use_global_device_ids=true | all-gather | bytes 126720 | tf_op jit(solution)/shard_map/all_gather | solution.py:177
  106.6 0.3 convolution_bitcast_fusion.1
  107.2 116.6 %all-gather = f32[240,18,32]{2,1,0:T(8,128)S(1)} all-gather(f32[5,18,32]{2,1,0:T(8,128)S(1)} %pad_maximum_fusion.2), channel_id=2, replica_groups=mesh['yy'=2,'lat'=24,'lon'=16] {'yy','lat'}, dimensions={0}, use_global_device_ids=true | all-gather | bytes 564480 | tf_op jit(solution)/shard_map/all_gather | solution.py:171
  223.9 2.1 fusion.4
  226.0 0.6 fusion.92
  226.6 0.4 concatenate.34
  227.0 0.8 fusion.85
  227.9 1.9 collective-permute-start.2
  229.8 6.2 %collective-permute-start.3 = (f32[5,3,2496]{2,1,0:T(4,128)}, f32[5,3,2496]{2,1,0:T(4,128)}, u32[]{:S(2)}, u32[]{:S(2)}) collective-permute-start(f32[5,3,2496]{2,1,0:T(4,128)} %get-tuple-element.128), channel_id=1, source_target_pairs={{16,0},{32,16},{48,32},{64,48},{80,64},{96,80},{112,96},{128,112},... | collective-permute-start | bytes 449288 | tf_op jit(solution)/shard_map/ppermute | solution.py:27
  236.0 0.6 multiply_cosine_fusion
  236.7 0.7 reshape.540
  237.5 0.7 reshape.539
  238.2 1.5 copy.59
  239.7 1.2 reshape.535
  241.0 0.7 and_reduce_fusion
  241.7 0.7 copy-done.4
  242.4 1.3 pad_maximum_fusion
  243.7 2.1 fusion.35
  245.8 7.2 %scatter.26 = f32[5,22,2496]{2,1,0:T(8,128)S(1)} dynamic-update-slice(f32[5,22,2496]{2,1,0:T(8,128)S(1)} %pad_maximum_fusion, f32[5,3,2304]{2,1,0:T(4,128)S(1)} %fusion.35, s32[]{:T(128)} %constant.310.clone.1, s32[]{:T(128)} %bitcast.12, s32[]{:T(128)} %bitcast.13) | dynamic-update-slice | bytes 276484 | tf_op jit(solution)/shard_map/scatter | solution.py:189
  253.2 5.5 %scatter.29 = f32[5,22,2496]{2,1,0:T(8,128)S(1)} dynamic-update-slice(f32[5,22,2496]{2,1,0:T(8,128)S(1)} %scatter.26, f32[5,3,2304]{2,1,0:T(4,128)S(1)} %slice_select_fusion.2, s32[]{:T(128)} %constant.310.clone.1, s32[]{:T(128)} %constant.326.clone.1, s32[]{:T(128)} %constant.312.clone.1) | dynamic-update-slice | bytes 276484 | tf_op jit(solution)/shard_map/scatter | solution.py:197
  258.8 0.8 scatter.30
  259.6 2.1 scatter.31
  261.8 2.3 fusion.29
  264.1 0.4 broadcast_multiply_fusion.1
  264.9 0.6 copy-done.6
  265.5 1.2 multiply_add_fusion
  266.7 2.4 reshape.541
  269.2 1.3 constant_dynamic-slice_fusion
  271.4 1.9 collective-permute-start.5
  273.3 3.9 collective-permute-start.4
  277.2 77.5 %all-gather.3 = f32[160,6,32]{2,1,0:T(8,128)S(1)} all-gather(f32[5,6,32]{2,1,0:T(8,128)S(1)} %pad_maximum_fusion.5), channel_id=5, replica_groups=mesh['yy'=2,'lat'=24,'lon'=16] {'yy','lon'}, dimensions={0}, use_global_device_ids=true | all-gather | bytes 126720 | tf_op jit(solution)/shard_map/all_gather | solution.py:177
  354.8 108.1 %all-gather.2 = f32[240,18,32]{2,1,0:T(8,128)S(1)} all-gather(f32[5,18,32]{2,1,0:T(8,128)S(1)} %pad_maximum_fusion.3), channel_id=4, replica_groups=mesh['yy'=2,'lat'=24,'lon'=16] {'yy','lat'}, dimensions={0}, use_global_device_ids=true | all-gather | bytes 564480 | tf_op jit(solution)/shard_map/all_gather | solution.py:171
  462.8 2.1 fusion.7
  464.9 0.3 convolution_bitcast_fusion
  465.3 0.4 concatenate.37
  465.7 0.9 fusion.84
  466.7 1.9 collective-permute-start.6
  468.6 6.0 %collective-permute-start.7 = (f32[5,3,2496]{2,1,0:T(4,128)}, f32[5,3,2496]{2,1,0:T(4,128)}, u32[]{:S(2)}, u32[]{:S(2)}) collective-permute-start(f32[5,3,2496]{2,1,0:T(4,128)} %get-tuple-element.126), channel_id=1, source_target_pairs={{16,0},{32,16},{48,32},{64,48},{80,64},{96,80},{112,96},{128,112},... | collective-permute-start | bytes 449288 | tf_op jit(solution)/shard_map/ppermute | solution.py:27
  474.7 0.7 reshape.546
  475.5 0.7 reshape.545
  476.3 1.5 copy.66
  477.7 0.5 reshape.543
  478.3 1.5 pad_maximum_fusion.1
  479.7 2.1 fusion.34
  481.8 7.2 %scatter.34 = f32[5,22,2496]{2,1,0:T(8,128)S(1)} dynamic-update-slice(f32[5,22,2496]{2,1,0:T(8,128)S(1)} %pad_maximum_fusion.1, f32[5,3,2304]{2,1,0:T(4,128)S(1)} %fusion.34, s32[]{:T(128)} %constant.310.clone.1, s32[]{:T(128)} %bitcast.12, s32[]{:T(128)} %bitcast.13) | dynamic-update-slice | bytes 276484 | tf_op jit(solution)/shard_map/scatter | solution.py:189
  489.2 5.5 %scatter.35 = f32[5,22,2496]{2,1,0:T(8,128)S(1)} dynamic-update-slice(f32[5,22,2496]{2,1,0:T(8,128)S(1)} %scatter.34, f32[5,3,2304]{2,1,0:T(4,128)S(1)} %slice_select_fusion, s32[]{:T(128)} %constant.310.clone.1, s32[]{:T(128)} %constant.326.clone.1, s32[]{:T(128)} %constant.312.clone.1) | dynamic-update-slice | bytes 276484 | tf_op jit(solution)/shard_map/scatter | solution.py:197
  494.8 0.8 scatter.36
  495.7 2.1 scatter.39
  497.8 2.3 fusion.21
  500.1 0.4 broadcast_multiply_fusion
  500.9 0.6 copy-done.7
  501.5 2.0 multiply_bitcast_fusion
  (131 shorter events, 3.3 us)
Async XLA Ops:
  0.0 22.5 %copy-start = (s32[2,1,24]{2,1,0:T(1,128)S(1)}, s32[2,1,24]{2,1,0:T(1,128)}, u32[]{:S(2)}) copy-start(s32[2,1,24]{2,1,0:T(1,128)} %param.34) | copy-start | bytes 580
  0.9 225.7 %collective-permute-start.1 = (f32[5,16,96]{2,1,0:T(8,128)S(1)}, f32[5,16,96]{2,1,0:T(8,128)S(1)}, u32[]{:S(2)}, u32[]{:S(2)}) collective-permute-start(f32[5,16,96]{2,1,0:T(8,128)S(1)} %get-tuple-element.131), channel_id=1, source_target_pairs={{1,0},{2,1},{3,2},{4,3},{5,4},{6,5},{7,6},{8,7},{9,8},{10,9},{11,1... | collective-permute-start | bytes 92168 | tf_op jit(solution)/shard_map/ppermute | solution.py:27
  7.1 219.5 %collective-permute-start = (f32[5,16,96]{2,1,0:T(8,128)S(1)}, f32[5,16,96]{2,1,0:T(8,128)S(1)}, u32[]{:S(2)}, u32[]{:S(2)}) collective-permute-start(f32[5,16,96]{2,1,0:T(8,128)S(1)} %get-tuple-element.132), channel_id=1, source_target_pairs={{0,1},{1,2},{2,3},{3,4},{4,5},{5,6},{6,7},{7,8},{8,9},{9,10},{10,1... | collective-permute-start | bytes 92168 | tf_op jit(solution)/shard_map/ppermute | solution.py:24
  9.1 97.5 %copy-start.33 = (pred[32]{0:T(512)(128)(4,1)}, pred[32]{0:T(512)(128)(4,1)S(1)}, u32[]{:S(2)}) copy-start(pred[32]{0:T(512)(128)(4,1)S(1)} %fusion.76) | copy-start | bytes 100
  9.1 214.8 %copy-start.14 = (pred[48]{0:T(512)(128)(4,1)}, pred[48]{0:T(512)(128)(4,1)S(1)}, u32[]{:S(2)}) copy-start(pred[48]{0:T(512)(128)(4,1)S(1)} %fusion.75) | copy-start | bytes 148
  17.2 89.9 %copy-start.17 = (f32[18]{0:T(128)}, f32[18]{0:T(128)S(1)}, u32[]{:S(2)}) copy-start(f32[18]{0:T(128)S(1)} %fusion.79) | copy-start | bytes 220
  17.9 89.2 %copy-start.19 = (f32[18]{0:T(128)}, f32[18]{0:T(128)S(1)}, u32[]{:S(2)}) copy-start(f32[18]{0:T(128)S(1)} %get-tuple-element.157) | copy-start | bytes 220
  17.9 89.2 %copy-start.21 = (f32[18]{0:T(128)}, f32[18]{0:T(128)S(1)}, u32[]{:S(2)}) copy-start(f32[18]{0:T(128)S(1)} %get-tuple-element.158) | copy-start | bytes 220
  18.6 8.3 %copy-start.27 = (f32[6]{0:T(128)}, f32[6]{0:T(128)S(1)}, u32[]{:S(2)}) copy-start(f32[6]{0:T(128)S(1)} %fusion.80) | copy-start | bytes 76
  19.3 7.6 %copy-start.29 = (f32[6]{0:T(128)}, f32[6]{0:T(128)S(1)}, u32[]{:S(2)}) copy-start(f32[6]{0:T(128)S(1)} %get-tuple-element.149) | copy-start | bytes 76
  19.4 7.6 %copy-start.31 = (f32[6]{0:T(128)}, f32[6]{0:T(128)S(1)}, u32[]{:S(2)}) copy-start(f32[6]{0:T(128)S(1)} %get-tuple-element.150) | copy-start | bytes 76
  19.4 3.2 copy-start.38
  22.5 3.7 copy-start.13
  22.5 4.1 copy-start.12
  106.6 0.5 copy-start.35
  223.9 2.1 copy-start.25
  223.9 2.7 copy-start.1
  227.9 13.8 %collective-permute-start.2 = (f32[5,3,2496]{2,1,0:T(4,128)}, f32[5,3,2496]{2,1,0:T(4,128)S(1)}, u32[]{:S(2)}, u32[]{:S(2)}) collective-permute-start(f32[5,3,2496]{2,1,0:T(4,128)} %get-tuple-element.127), channel_id=1, source_target_pairs={{0,16},{16,32},{32,48},{48,64},{64,80},{80,96},{96,112},{112,128},... | collective-permute-start | bytes 449288 | tf_op jit(solution)/shard_map/ppermute | solution.py:24
  229.8 12.6 %collective-permute-start.3 = (f32[5,3,2496]{2,1,0:T(4,128)}, f32[5,3,2496]{2,1,0:T(4,128)}, u32[]{:S(2)}, u32[]{:S(2)}) collective-permute-start(f32[5,3,2496]{2,1,0:T(4,128)} %get-tuple-element.128), channel_id=1, source_target_pairs={{16,0},{32,16},{48,32},{64,48},{80,64},{96,80},{112,96},{128,112},... | collective-permute-start | bytes 449288 | tf_op jit(solution)/shard_map/ppermute | solution.py:27
  239.7 1.2 copy-start.37
  241.7 2.0 copy-start.3
  241.7 0.7 copy-start.4
  242.4 1.3 copy-start.5
  243.7 15.1 %copy-start.11 = (f32[5,16,96]{2,1,0:T(8,128)S(1)}, f32[5,16,96]{2,1,0:T(8,128)}, u32[]{:S(2)}) copy-start(f32[5,16,96]{2,1,0:T(8,128)} %reshape.539) | copy-start | bytes 92164
  243.7 15.9 %copy-start.9 = (f32[5,16,96]{2,1,0:T(8,128)S(1)}, f32[5,16,96]{2,1,0:T(8,128)}, u32[]{:S(2)}) copy-start(f32[5,16,96]{2,1,0:T(8,128)} %reshape.540) | copy-start | bytes 92164
  243.7 18.1 %copy-start.23 = (f32[16]{0:T(128)S(1)}, f32[16]{0:T(128)}, u32[]{:S(2)}) copy-start(f32[16]{0:T(128)} %get-tuple-element.159) | copy-start | bytes 196
  264.6 0.9 copy-start.6
  264.6 0.9 copy-start.16
  269.2 1.7 copy-start.28
  269.2 1.7 copy-start.30
  269.2 1.7 copy-start.32
  269.2 2.1 copy-start.18
  269.2 2.1 copy-start.20
  269.2 2.1 copy-start.22
  271.4 193.9 %collective-permute-start.5 = (f32[5,16,96]{2,1,0:T(8,128)S(1)}, f32[5,16,96]{2,1,0:T(8,128)S(1)}, u32[]{:S(2)}, u32[]{:S(2)}) collective-permute-start(f32[5,16,96]{2,1,0:T(8,128)S(1)} %get-tuple-element.129), channel_id=1, source_target_pairs={{1,0},{2,1},{3,2},{4,3},{5,4},{6,5},{7,6},{8,7},{9,8},{10,9},{11,1... | collective-permute-start | bytes 92168 | tf_op jit(solution)/shard_map/ppermute | solution.py:27
  273.3 192.0 %collective-permute-start.4 = (f32[5,16,96]{2,1,0:T(8,128)S(1)}, f32[5,16,96]{2,1,0:T(8,128)S(1)}, u32[]{:S(2)}, u32[]{:S(2)}) collective-permute-start(f32[5,16,96]{2,1,0:T(8,128)S(1)} %get-tuple-element.130), channel_id=1, source_target_pairs={{0,1},{1,2},{2,3},{3,4},{4,5},{5,6},{6,7},{7,8},{8,9},{9,10},{10,1... | collective-permute-start | bytes 92168 | tf_op jit(solution)/shard_map/ppermute | solution.py:24
  354.7 108.1 %copy-start.15 = (pred[48]{0:T(512)(128)(4,1)S(1)}, pred[48]{0:T(512)(128)(4,1)}, u32[]{:S(2)}) copy-start(pred[48]{0:T(512)(128)(4,1)} %copy-done.14) | copy-start | bytes 148
  354.7 108.1 %copy-start.26 = (s32[48]{0:T(128)S(1)}, s32[48]{0:T(128)}, u32[]{:S(2)}) copy-start(s32[48]{0:T(128)} %copy-done.25) | copy-start | bytes 580
  462.8 2.1 copy-start.34
  462.8 2.1 copy-start.36
  465.7 9.8 %copy-start.2 = (f32[5,16,2496]{2,1,0:T(8,128)}, f32[5,16,2496]{2,1,0:T(8,128)S(1)}, u32[]{:S(2)}) copy-start(f32[5,16,2496]{2,1,0:T(8,128)S(1)} %concatenate.37) | copy-start | bytes 2396164
  466.7 11.6 %collective-permute-start.6 = (f32[5,3,2496]{2,1,0:T(4,128)}, f32[5,3,2496]{2,1,0:T(4,128)S(1)}, u32[]{:S(2)}, u32[]{:S(2)}) collective-permute-start(f32[5,3,2496]{2,1,0:T(4,128)} %get-tuple-element.125), channel_id=1, source_target_pairs={{0,16},{16,32},{32,48},{48,64},{64,80},{80,96},{96,112},{112,128},... | collective-permute-start | bytes 449288 | tf_op jit(solution)/shard_map/ppermute | solution.py:24
  468.6 9.7 %collective-permute-start.7 = (f32[5,3,2496]{2,1,0:T(4,128)}, f32[5,3,2496]{2,1,0:T(4,128)}, u32[]{:S(2)}, u32[]{:S(2)}) collective-permute-start(f32[5,3,2496]{2,1,0:T(4,128)} %get-tuple-element.126), channel_id=1, source_target_pairs={{16,0},{32,16},{48,32},{64,48},{80,64},{96,80},{112,96},{128,112},... | collective-permute-start | bytes 449288 | tf_op jit(solution)/shard_map/ppermute | solution.py:27
  479.7 15.9 %copy-start.8 = (f32[5,16,96]{2,1,0:T(8,128)S(1)}, f32[5,16,96]{2,1,0:T(8,128)}, u32[]{:S(2)}) copy-start(f32[5,16,96]{2,1,0:T(8,128)} %reshape.546) | copy-start | bytes 92164
  479.7 18.1 %copy-start.24 = (f32[16]{0:T(128)S(1)}, f32[16]{0:T(128)}, u32[]{:S(2)}) copy-start(f32[16]{0:T(128)} %get-tuple-element.159) | copy-start | bytes 196
  481.8 12.9 %copy-start.10 = (f32[5,16,96]{2,1,0:T(8,128)S(1)}, f32[5,16,96]{2,1,0:T(8,128)}, u32[]{:S(2)}) copy-start(f32[5,16,96]{2,1,0:T(8,128)} %reshape.545) | copy-start | bytes 92164
  500.6 0.9 copy-start.7
where the time goes:
time: 504 us
  blocking collectives  382 us (76%)
  local copies, waits for them, and re-layouts  57.8 us (11%)
  starting transfers between devices  30 us (6%)
  other arithmetic  20 us (4%)
  between operations  8.06 us (2%)
  matrix products  5.98 us (1%)
    all_gather x2, blocking collectives, section_rate(): lax.all_gather(lat_part[None], ('yy', 'lat'), axis=0, tiled=True)  225 us
    all_gather x2, blocking collectives, section_rate(): lax.all_gather(lon_part[None], ('yy', 'lon'), axis=0, tiled=True)  157 us
    ppermute x4, starting transfers between devices, extended(): lax.ppermute(lax.slice_in_dim(block, 0, width, axis=dim), axis, backward)  20.4 us
    scatter x2, local copies, waits for them, and re-layouts, section_rate(): padded.at[:, 0:3, edge_width:edge_width + merged_width].set(ghost_south)  14.4 us
    scatter x2, local copies, waits for them, and re-layouts, section_rate(): padded = padded.at[:, tile_rows + 3:tile_rows + 6, edge_width:edge_width...  11 us
  transfers between devices with their start and end apart: 8, of which 0 were waited for; matrix products, arithmetic and copies ran while one was open for 5% of the time, Pallas kernels for 0%

commit v1 on v0

v1 whole, which is shorter than its diff:
```python
import math

import jax
import jax.numpy as jnp
from jax import lax
from jax.experimental import pallas as pl
from jax.experimental.pallas import tpu as pltpu
from jax.sharding import PartitionSpec as P

FIELDS = 5
LEV = 32
CLAT = 16
GROUPS = 18
LANES = 128
PATCH_H = 8
PATCH_W = 16
LAT_BLOCK = 18
LON_BLOCK = 6
SPAN = 5
TOP = 8

TIME_STEP = 0.2
KAPPA_PRESS = 0.4
GAMMA_HEAT = 1.4

MESH = pl.DeviceIdType.MESH
HIGHEST = lax.Precision.HIGHEST


def dot(left, right):
    return jnp.dot(left, right, precision=HIGHEST, preferred_element_type=jnp.float32)


def iota(shape, axis):
    return lax.broadcasted_iota(jnp.int32, shape, axis)


def kernel(
    n_lat,
    n_lon,
    fields,
    visc,
    lat_w,
    lon_w,
    lat_ang,
    lon_ang,
    rows,
    cols,
    lat_pair,
    lon_pair,
    out,
    x1,
    x2,
    wp,
    mat,
    zbuf,
    wbuf,
    rl,
    rw,
    halo_send,
    halo_recv,
    rim_send,
    rim_recv,
):
    p = lax.axis_index("yy")
    a = lax.axis_index("lat")
    b = lax.axis_index("lon")
    q = 1 - p
    low_a, high_a = a == 0, a == n_lat - 1
    low_b, high_b = b == 0, b == n_lon - 1
    neighbours = (
        (jnp.logical_not(low_a), (p, a - 1, b)),
        (jnp.logical_not(high_a), (p, a + 1, b)),
        (jnp.logical_not(low_b), (p, a, b - 1)),
        (jnp.logical_not(high_b), (p, a, b + 1)),
    )

    barrier = pltpu.get_barrier_semaphore()
    for there, device in neighbours:

        @pl.when(there)
        def _():
            pl.semaphore_signal(barrier, inc=1, device_id=device, device_id_type=MESH)

    @pl.when(jnp.logical_or(low_a, high_a))
    def _():
        def one(i, carry):
            pl.semaphore_signal(barrier, inc=1, device_id=(q, i, b), device_id_type=MESH)
            return carry

        lax.fori_loop(0, n_lat, one, 0)

    @pl.when(jnp.logical_or(low_b, high_b))
    def _():
        def one(i, carry):
            pl.semaphore_signal(barrier, inc=1, device_id=(q, a, i), device_id_type=MESH)
            return carry

        lax.fori_loop(0, n_lon, one, 0)

    for f in range(FIELDS):
        for g in range(GROUPS):
            x1[f, g + 1, TOP : TOP + CLAT, :] = fields[0, f, :, g * LANES : (g + 1) * LANES]

    wp[...] = jnp.zeros_like(wp)
    for t in range(LAT_BLOCK):
        u, v = t // 4, t % 4
        wp[0, v * 8 + u : v * 8 + u + 1, :] = lat_w[0, 0, 0, t : t + 1, :]
    for t in range(LON_BLOCK):
        u, v = (5, t + 1) if t < 3 else (6, t - 3)
        wp[1, v * 8 + u : v * 8 + u + 1, :] = lon_w[0, 0, 0, t : t + 1, :]
    entry = iota((LANES, GROUPS * CLAT), 0)
    place = iota((LANES, GROUPS * CLAT), 1)
    entry_row, entry_col = entry >> 4, entry & (PATCH_W - 1)
    place_row, place_col = place & (CLAT - 1), 4 * (place >> 4)
    same_row, from_col = [], []
    for j in range(2):
        same_row.append(place_row - entry_row == rows[0, 0, 0, j])
        from_col.append(entry_col - place_col + cols[0, 0, 0, j])
    for kk in range(4):
        part = None
        for j in range(2):
            chosen = jnp.where(jnp.logical_and(same_row[j], from_col[j] == kk), 1.0, 0.0)
            term = dot(wp[j], chosen)
            part = term if part is None else part + term
        mat[kk * 32 : (kk + 1) * 32, :] = part

    lane = iota((8, LANES), 1)
    sub = iota((8, LANES), 0)
    lane_group = lane >> 5
    target = 4 * sub + lane_group
    angle = jnp.zeros((8, LANES), jnp.float32)
    for t in range(LAT_BLOCK):
        angle = jnp.where(target == t, lat_ang[0, 0, 0, t], angle)
    for t in range(LON_BLOCK):
        u, v = (5, t + 1) if t < 3 else (6, t - 3)
        angle = jnp.where(target == 4 * u + v, lon_ang[0, 0, 0, t], angle)
    cos_angle = jnp.cos(angle)
    sin_angle = jnp.sin(angle)

    total_rows = CLAT * n_lat
    inv_lon, inv_sq = [], []
    for h in range(2):
        row = (a * CLAT + 8 * h + sub).astype(jnp.float32)
        cosine = jnp.cos((row + 0.5 - 0.5 * total_rows) * (0.5 * math.pi / total_rows))
        inv_lon.append(1.0 / (60.0 * cosine))
        inv_sq.append(1.0 / (cosine * cosine))

    k_lat = 4 * (iota((32, n_lat), 0) & 7) + (iota((32, n_lat), 0) >> 3) + jnp.where(low_a, 0, n_lat // 2)
    choose_lat = jnp.where(lat_pair[p] == k_lat, 1.0, 0.0)
    choose_lon = jnp.where(lon_pair[p] == iota((CLAT, n_lon), 0), 1.0, 0.0)

    count = 4
    for there, _ in neighbours:
        count = count + jnp.where(there, 1, 0)
    pl.semaphore_wait(barrier, count)

    def halo_copies(s, x):
        inner = pl.ds(1, GROUPS)
        pieces = (
            (x.at[:, inner, pl.ds(TOP, 3), :], x.at[:, inner, pl.ds(TOP + CLAT, 3), :]),
            (x.at[:, inner, pl.ds(TOP + CLAT - 3, 3), :], x.at[:, inner, pl.ds(TOP - 3, 3), :]),
            (x.at[:, 1, pl.ds(TOP, CLAT), :], x.at[:, GROUPS + 1, pl.ds(TOP, CLAT), :]),
            (x.at[:, GROUPS, pl.ds(TOP, CLAT), :], x.at[:, 0, pl.ds(TOP, CLAT), :]),
        )
        copies = []
        for i, ((there, device), (src, dst)) in enumerate(zip(neighbours, pieces)):
            copies.append(
                (
                    there,
                    pltpu.make_async_remote_copy(
                        src_ref=src,
                        dst_ref=dst,
                        send_sem=halo_send.at[s, i],
                        recv_sem=halo_recv.at[s, i],
                        device_id=device,
                        device_id_type=MESH,
                    ),
                )
            )
        return copies

    def rim_copies(s):
        lat_src = zbuf.at[s, :, pl.ds(0, SPAN), :]
        lat_dst = rl.at[s, a]
        ends = (
            (lat_src, lat_dst.at[:, pl.ds(0, SPAN), :], (q, 0, b), 0),
            (lat_src, lat_dst.at[:, pl.ds(0, SPAN), :], (q, n_lat - 1, b), 0),
            (wbuf.at[s, 0], rw.at[s, b], (q, a, 0), 1),
            (wbuf.at[s, 1], rw.at[s, b], (q, a, n_lon - 1), 1),
        )
        return [
            pltpu.make_async_remote_copy(
                src_ref=src,
                dst_ref=dst,
                send_sem=rim_send.at[s, i],
                recv_sem=rim_recv.at[s, kind],
                device_id=device,
                device_id_type=MESH,
            )
            for i, (src, dst, device, kind) in enumerate(ends)
        ]

    def export(s, x):
        columns = []
        for f in range(FIELDS):
            parts = [x[f, g + 1, TOP : TOP + CLAT, :] for g in range(GROUPS)]
            columns.append(jnp.concatenate(parts, axis=0))
        total = dot(mat[...], jnp.concatenate(columns, axis=1))
        blocks = []
        for f in range(FIELDS):
            piece = total[:, f * LANES : (f + 1) * LANES]
            result = None
            for shift in range(4):
                mixed = None
                for kk in range(4):
                    v = (kk + shift) % 4
                    part = piece[kk * 32 + v * 8 : kk * 32 + v * 8 + 8, :]
                    mixed = part if mixed is None else jnp.where(lane_group == kk, part, mixed)
                if shift:
                    mixed = pltpu.roll(mixed, 32 * shift, 1)
                result = mixed if result is None else result + mixed
            blocks.append(result)
        east = cos_angle * blocks[1] + sin_angle * blocks[2]
        north = cos_angle * blocks[2] - sin_angle * blocks[1]
        blocks[1], blocks[2] = east, north
        for f in range(FIELDS):
            zbuf[s, f] = blocks[f]
            wbuf[s, 0, f : f + 1, :] = blocks[f][5:6]
            wbuf[s, 1, f : f + 1, :] = blocks[f][6:7]

    def place_lat(s, x, first_row):
        half = lane < 64
        for f in range(FIELDS):
            got = []
            for u in range(SPAN):
                got.append(jnp.concatenate([rl[s, i, f, u : u + 1, :] for i in range(n_lat)], axis=0))
            placed = dot(choose_lat, jnp.concatenate(got, axis=1))
            for c in range(2):
                plain = [placed[16 * c : 16 * c + 8, u * LANES : (u + 1) * LANES] for u in range(SPAN)]
                moved = [
                    pltpu.roll(placed[16 * c + 8 : 16 * c + 16, u * LANES : (u + 1) * LANES], 64, 1)
                    for u in range(SPAN)
                ]
                tiles = plain[:4] + [jnp.where(half, plain[4], moved[0])]
                tiles += [jnp.where(half, moved[u], moved[u + 1]) for u in range(4)]
                for g, value in enumerate(tiles):
                    x[f, 1 + 9 * c + g, first_row : first_row + 3, :] = value[0:3]

    def place_lon(s, x, group):
        got = []
        for f in range(FIELDS):
            got.append(jnp.concatenate([rw[s, i, f : f + 1, :] for i in range(n_lon)], axis=0))
        placed = dot(choose_lon, jnp.concatenate(got, axis=1))
        for f in range(FIELDS):
            x[f, group, TOP : TOP + CLAT, :] = placed[:, f * LANES : (f + 1) * LANES]

    def receive(s, x):
        lat_got = rl.at[s, :, :, pl.ds(0, SPAN), :]
        lon_got = rw.at[s]

        @pl.when(jnp.logical_or(low_b, high_b))
        def _():
            pltpu.make_async_copy(lon_got, lon_got, rim_recv.at[s, 1]).wait()

        @pl.when(low_b)
        def _():
            place_lon(s, x, 0)

        @pl.when(high_b)
        def _():
            place_lon(s, x, GROUPS + 1)

        @pl.when(jnp.logical_or(low_a, high_a))
        def _():
            pltpu.make_async_copy(lat_got, lat_got, rim_recv.at[s, 0]).wait()

        @pl.when(low_a)
        def _():
            place_lat(s, x, TOP - 3)

        @pl.when(high_a)
        def _():
            place_lat(s, x, TOP + CLAT)

    not_last = (lane & (LEV - 1)) != LEV - 1
    not_first = (lane & (LEV - 1)) != 0

    def derivatives(x, f, g, r, h):
        def row(o):
            return x[f, g, r + o : r + o + 8, :]

        here = row(0)
        west, east = x[f, g - 1, r : r + 8, :], x[f, g + 1, r : r + 8, :]
        up1, down1 = row(1), row(-1)
        lat = (
            0.75 * (up1 - down1) - 0.15 * (row(2) - row(-2)) + (1.0 / 60.0) * (row(3) - row(-3))
        )
        plus1 = pltpu.roll(jnp.where(lane < 32, east, here), 96, 1)
        minus1 = pltpu.roll(jnp.where(lane >= 96, west, here), 32, 1)
        two = pltpu.roll(jnp.where(lane < 64, east - here, here - west), 64, 1)
        plus3 = pltpu.roll(jnp.where(lane < 96, east, here), 32, 1)
        minus3 = pltpu.roll(jnp.where(lane >= 32, west, here), 96, 1)
        lon = (45.0 * (plus1 - minus1) - 9.0 * two + (plus3 - minus3)) * inv_lon[h]
        upper = jnp.where(not_last, pltpu.roll(here, LANES - 1, 1), 0.0)
        lower = jnp.where(not_first, pltpu.roll(here, 1, 1), 0.0)
        lev = 0.5 * (upper - lower)
        lap = up1 + down1 - 2.0 * here + (plus1 + minus1 - 2.0 * here) * inv_sq[h]
        return here, lat, lon, lev, lap

    def section(x, store):
        def step(g, carry):
            begin = pl.multiple_of((g - 1) * LANES, LANES)
            for h in range(2):
                r = TOP + 8 * h
                u = x[1, g, r : r + 8, :]
                v = x[2, g, r : r + 8, :]
                w = x[3, g, r : r + 8, :]
                rho = x[0, g, r : r + 8, :]
                nu = visc[0, 8 * h : 8 * h + 8, pl.ds(begin, LANES)]

                def plain(f):
                    here, lat, lon, lev, lap = derivatives(x, f, g, r, h)
                    return here, lat, lon, lev, nu * lap - (u * lon + v * lat + w * lev)

                e, e_lat, e_lon, e_lev, e_rate = plain(4)
                here, _, lon, _, rate = plain(1)
                div = lon
                store(1, g, h, begin, here, rate - KAPPA_PRESS * e_lon)
                here, lat, _, _, rate = plain(2)
                div = div + lat
                store(2, g, h, begin, here, rate - KAPPA_PRESS * e_lat)
                here, _, _, lev, rate = plain(3)
                div = div + lev
                store(3, g, h, begin, here, rate - KAPPA_PRESS * e_lev - rho)
                here, _, _, _, rate = plain(0)
                store(0, g, h, begin, here, rate - div)
                store(4, g, h, begin, e, e_rate - GAMMA_HEAT * div)
            return carry

        lax.fori_loop(1, GROUPS + 1, step, 0)

    def store_first(f, g, h, begin, here, rate):
        x2[f, g, TOP + 8 * h : TOP + 8 * h + 8, :] = here + TIME_STEP * rate

    def store_second(f, g, h, begin, here, rate):
        before = x1[f, g, TOP + 8 * h : TOP + 8 * h + 8, :]
        out[0, f, 8 * h : 8 * h + 8, pl.ds(begin, LANES)] = 0.5 * (
            before + here + TIME_STEP * rate
        )

    def exchange(s, x):
        halos = halo_copies(s, x)
        for there, copy in halos:

            @pl.when(there)
            def _():
                copy.start()

        export(s, x)
        rims = rim_copies(s)
        for copy in rims:
            copy.start()
        for there, copy in halos:

            @pl.when(there)
            def _():
                copy.wait_send()

        for i in range(4):
            there, _ = neighbours[i]
            copy = halos[i ^ 1][1]

            @pl.when(there)
            def _():
                copy.wait_recv()

        receive(s, x)
        for copy in rims:
            copy.wait_send()

    exchange(0, x1)
    section(x1, store_first)
    exchange(1, x2)
    section(x2, store_second)


def on_device(*operands):
    n_lat = lax.axis_size("lat")
    n_lon = lax.axis_size("lon")
    vmem = pl.BlockSpec(memory_space=pltpu.VMEM)
    smem = pl.BlockSpec(memory_space=pltpu.SMEM)

    def body(*refs):
        kernel(n_lat, n_lon, *refs)

    return pl.pallas_call(
        body,
        out_shape=jax.ShapeDtypeStruct(operands[0].shape, jnp.float32),
        in_specs=[vmem, vmem, vmem, vmem, smem, smem, smem, smem, vmem, vmem],
        out_specs=vmem,
        scratch_shapes=[
            pltpu.VMEM((FIELDS, GROUPS + 2, 32, LANES), jnp.float32),
            pltpu.VMEM((FIELDS, GROUPS + 2, 32, LANES), jnp.float32),
            pltpu.VMEM((2, 32, LANES), jnp.float32),
            pltpu.VMEM((LANES, GROUPS * CLAT), jnp.float32),
            pltpu.VMEM((2, FIELDS, 8, LANES), jnp.float32),
            pltpu.VMEM((2, 2, 8, LANES), jnp.float32),
            pltpu.VMEM((2, n_lat, FIELDS, 8, LANES), jnp.float32),
            pltpu.VMEM((2, n_lon, 8, LANES), jnp.float32),
            pltpu.SemaphoreType.DMA((2, 4)),
            pltpu.SemaphoreType.DMA((2, 4)),
            pltpu.SemaphoreType.DMA((2, 4)),
            pltpu.SemaphoreType.DMA((2, 2)),
        ],
        compiler_params=pltpu.CompilerParams(
            collective_id=0, has_side_effects=True, vmem_limit_bytes=40 * 1024 * 1024
        ),
    )(*operands)


def solution(mesh):
    in_specs = (
        P("yy", None, "lat", "lon"),
        P("yy", "lat", "lon"),
        P("yy", "lat", "lon", None, None),
        P("yy", "lat", "lon", None, None),
        P("yy", "lat", "lon", None),
        P("yy", "lat", "lon", None),
        P("yy", "lat", "lon", None),
        P("yy", "lat", "lon", None),
        P(None, "lon", None),
        P(None, "lat", None),
    )
    out_specs = P("yy", None, "lat", "lon")
    return jax.shard_map(
        on_device, mesh=mesh, in_specs=in_specs, out_specs=out_specs, check_vma=False
    )
```

time: 504 us -> 48.7 us (0.10)
  the two profiles are of different devices: /device:TPU:6 before, /device:TPU:1 now
where the time goes in v1:
time: 48.7 us; the launch traced here: 48.4 us
  Pallas kernels  44 us (90%)
  local copies, waits for them, and re-layouts  4.36 us (9%)
    pallas_call x1, Pallas kernels, on_device(): pl.pallas_call(body, out_shape=jax.ShapeDtypeStruct(operands[0].shape, jn...  44 us
    unnamed x19, local copies, waits for them, and re-layouts  4.36 us

profile of v1, /device:TPU:1, one launch (start us, length us, event | category | flops | bytes accessed | tf_op | source)
XLA Modules:
  0.0 48.4 jit_solution(12581521597317725947)
XLA Ops:
  0.0 0.7 %copy.12.refs_3_ = f32[1,1,1,6,128]{4,3,2,1,0:T(8,128)S(1)} copy(f32[1,1,1,6,128]{4,2,3,1,0:T(1,128)} %param.13) | data formatting | bytes 6144 | tf_op args[3]
  0.7 0.0 copy-start.2
  0.7 0.0 copy-start.3
  0.7 0.0 copy-start.4
  0.7 0.0 copy-start.5
  0.7 0.0 copy-start.6
  0.7 0.0 copy-start.7
  0.7 0.8 %copy.11.refs_2_ = f32[1,1,1,18,128]{4,3,2,1,0:T(8,128)S(1)} copy(f32[1,1,1,18,128]{4,2,3,1,0:T(1,128)} %param.12) | data formatting | bytes 18432 | tf_op args[2]
  1.5 0.0 copy-done.2
  1.5 0.0 copy-done.3
  1.5 0.0 copy-done.4
  1.5 0.0 copy-done.5
  1.5 0.0 copy-done.6
  1.5 0.0 copy-done.7
  1.5 0.0 copy-start
  1.5 1.1 %copy-done = f32[1,5,16,2304]{3,2,1,0:T(8,128)S(1)} copy-done((f32[1,5,16,2304]{3,2,1,0:T(8,128)S(1)}, f32[1,5,16,2304]{3,2,1,0:T(8,128)}, u32[]{:S(2)}) %copy-start) | copy-done | bytes 737304
  2.6 0.0 copy-start.1
  2.6 0.9 %copy-done.1 = f32[1,16,2304]{2,1,0:T(8,128)S(1)} copy-done((f32[1,16,2304]{2,1,0:T(8,128)S(1)}, f32[1,16,2304]{2,1,0:T(8,128)}, u32[]{:S(2)}) %copy-start.1) | copy-done | bytes 147480
  3.6 44.0 %shard_map.100 = f32[1,5,16,2304]{3,2,1,0:T(8,128)S(1)} custom-call(f32[1,5,16,2304]{3,2,1,0:T(8,128)S(1)} %copy-done, f32[1,16,2304]{2,1,0:T(8,128)S(1)} %copy-done.1, f32[1,1,1,18,128]{4,3,2,1,0:T(8,128)S(1)} %copy.11.refs_2_, f32[1,1,1,6,128]{4,3,2,1,0:T(8,128)S(1)} %copy.12.refs_3_, f32[1,1,1,18]{3,2,1,0:T(1,128)S(1)} %copy-done.4, ...), custom_call_target="tpu_custom_call" | custom-call | tf_op jit(solution)/shard_map/pallas_call | solution.py:397
  47.6 0.9 %copy.14 = f32[1,5,16,2304]{3,2,1,0:T(8,128)} copy(f32[1,5,16,2304]{3,2,1,0:T(8,128)S(1)} %shard_map.100) | data formatting | bytes 1474560
Async XLA Ops:
  0.7 0.8 %copy-start.2 = (s32[2,1,24]{2,1,0:T(1,128)S(1)}, s32[2,1,24]{2,1,0:T(1,128)}, u32[]{:S(2)}) copy-start(s32[2,1,24]{2,1,0:T(1,128)} %refs_8_.1) | copy-start | bytes 580
  0.7 0.8 %copy-start.3 = (s32[2,1,16]{2,1,0:T(1,128)S(1)}, s32[2,1,16]{2,1,0:T(1,128)}, u32[]{:S(2)}) copy-start(s32[2,1,16]{2,1,0:T(1,128)} %refs_9_.1) | copy-start | bytes 388
  0.7 0.8 %copy-start.4 = (f32[1,1,1,18]{3,2,1,0:T(1,128)S(1)}, f32[1,1,1,18]{3,2,1,0:T(1,128)}, u32[]{:S(2)}) copy-start(f32[1,1,1,18]{3,2,1,0:T(1,128)} %refs_4_.1) | copy-start | bytes 220
  0.7 0.8 %copy-start.5 = (f32[1,1,1,6]{3,2,1,0:T(1,128)S(1)}, f32[1,1,1,6]{3,2,1,0:T(1,128)}, u32[]{:S(2)}) copy-start(f32[1,1,1,6]{3,2,1,0:T(1,128)} %refs_5_.1) | copy-start | bytes 76
  0.7 0.8 %copy-start.6 = (s32[1,1,1,2]{3,2,1,0:T(1,128)S(1)}, s32[1,1,1,2]{3,2,1,0:T(1,128)}, u32[]{:S(2)}) copy-start(s32[1,1,1,2]{3,2,1,0:T(1,128)} %refs_6_.1) | copy-start | bytes 28
  0.7 0.8 %copy-start.7 = (s32[1,1,1,2]{3,2,1,0:T(1,128)S(1)}, s32[1,1,1,2]{3,2,1,0:T(1,128)}, u32[]{:S(2)}) copy-start(s32[1,1,1,2]{3,2,1,0:T(1,128)} %refs_7_.1) | copy-start | bytes 28
  1.5 1.1 %copy-start = (f32[1,5,16,2304]{3,2,1,0:T(8,128)S(1)}, f32[1,5,16,2304]{3,2,1,0:T(8,128)}, u32[]{:S(2)}) copy-start(f32[1,5,16,2304]{3,2,1,0:T(8,128)} %refs_0_.1) | copy-start | bytes 2211844
  2.6 0.9 %copy-start.1 = (f32[1,16,2304]{2,1,0:T(8,128)S(1)}, f32[1,16,2304]{2,1,0:T(8,128)}, u32[]{:S(2)}) copy-start(f32[1,16,2304]{2,1,0:T(8,128)} %refs_1_.1) | copy-start | bytes 442372

commit v2 on v1

v2 whole, which is shorter than its diff:
```python
import math

import jax
import jax.numpy as jnp
from jax import lax
from jax.experimental import pallas as pl
from jax.experimental.pallas import tpu as pltpu
from jax.sharding import PartitionSpec as P

FIELDS = 5
LEV = 32
CLAT = 16
GROUPS = 18
LANES = 128
PATCH_H = 8
PATCH_W = 16
LAT_BLOCK = 18
LON_BLOCK = 6
SPAN = 5
BLOCK_ROWS = 32
TOP = 8

TIME_STEP = 0.2
KAPPA_PRESS = 0.4
GAMMA_HEAT = 1.4

MESH = pl.DeviceIdType.MESH


def dot(left, right):
    return jnp.dot(left, right, preferred_element_type=jnp.float32)


def iota(shape, axis):
    return lax.broadcasted_iota(jnp.int32, shape, axis)


def split(value, parts):
    pieces = []
    for _ in range(parts):
        piece = value.astype(jnp.bfloat16)
        pieces.append(piece)
        value = value - piece.astype(jnp.float32)
    return pieces


def kernel(
    n_lat,
    n_lon,
    fields_hbm,
    visc_hbm,
    lat_w_hbm,
    lon_w_hbm,
    lat_ang_hbm,
    lon_ang_hbm,
    rows_hbm,
    cols_hbm,
    lat_pair_hbm,
    lon_pair_hbm,
    out,
    x1,
    x2,
    visc,
    lat_w,
    lon_w,
    lat_ang,
    lon_ang,
    rows,
    cols,
    lat_pair,
    lon_pair,
    wp,
    mat,
    metric,
    zbuf,
    wbuf,
    rl,
    rw,
    local,
    halo_send,
    halo_recv,
    rim_send,
    rim_recv,
):
    p = lax.axis_index("yy")
    a = lax.axis_index("lat")
    b = lax.axis_index("lon")
    q = 1 - p
    low_a, high_a = a == 0, a == n_lat - 1
    low_b, high_b = b == 0, b == n_lon - 1
    lat_edge = jnp.logical_or(low_a, high_a)
    lon_edge = jnp.logical_or(low_b, high_b)
    neighbours = (
        (jnp.logical_not(low_a), (p, a - 1, b)),
        (jnp.logical_not(high_a), (p, a + 1, b)),
        (jnp.logical_not(low_b), (p, a, b - 1)),
        (jnp.logical_not(high_b), (p, a, b + 1)),
    )

    small = [
        pltpu.make_async_copy(src, dst, local.at[i])
        for i, (src, dst) in enumerate(
            (
                (lat_w_hbm, lat_w),
                (lon_w_hbm, lon_w),
                (lat_ang_hbm, lat_ang),
                (lon_ang_hbm, lon_ang),
                (rows_hbm, rows),
                (cols_hbm, cols),
                (lat_pair_hbm, lat_pair),
                (lon_pair_hbm, lon_pair),
                (visc_hbm, visc),
            )
        )
    ]
    for copy in small[:6]:
        copy.start()
    inner = pl.ds(1, GROUPS)
    for g in range(GROUPS):
        pltpu.make_async_copy(
            fields_hbm.at[0, :, :, pl.ds(g * LANES, LANES)],
            x1.at[:, g + 1, pl.ds(TOP, CLAT), :],
            local.at[9],
        ).start()
    for copy in small[6:]:
        copy.start()

    barrier = pltpu.get_barrier_semaphore()
    for there, device in neighbours:

        @pl.when(there)
        def _():
            pl.semaphore_signal(barrier, inc=1, device_id=device, device_id_type=MESH)

    @pl.when(lat_edge)
    def _():
        def one(i, carry):
            pl.semaphore_signal(barrier, inc=1, device_id=(q, i, b), device_id_type=MESH)
            return carry

        lax.fori_loop(0, n_lat, one, 0)

    @pl.when(lon_edge)
    def _():
        def one(i, carry):
            pl.semaphore_signal(barrier, inc=1, device_id=(q, a, i), device_id_type=MESH)
            return carry

        lax.fori_loop(0, n_lon, one, 0)

    wp[...] = jnp.zeros_like(wp)
    for copy in small[:6]:
        copy.wait()
    for t in range(LAT_BLOCK):
        u, v = t // 4, t % 4
        wp[v * 8 + u : v * 8 + u + 1, 0:LANES] = lat_w[t]
    for t in range(LON_BLOCK):
        u, v = (5, t + 1) if t < 3 else (6, t - 3)
        wp[v * 8 + u : v * 8 + u + 1, LANES : 2 * LANES] = lon_w[t]
    weights = jnp.concatenate(split(wp[...], 3), axis=0)
    entry = iota((2 * LANES, GROUPS * CLAT), 0)
    place = iota((2 * LANES, GROUPS * CLAT), 1)
    is_lon = entry >= LANES
    entry = entry & (LANES - 1)
    row0 = jnp.where(is_lon, rows[0, 0, 0, 1], rows[0, 0, 0, 0])
    col0 = jnp.where(is_lon, cols[0, 0, 0, 1], cols[0, 0, 0, 0])
    from_col = (entry & (PATCH_W - 1)) - 4 * (place >> 4) + col0
    same_row = (place & (CLAT - 1)) - (entry >> 4) == row0
    from_col = jnp.where(same_row, from_col, -1)
    for kk in range(4):
        chosen = jnp.where(from_col == kk, 1.0, 0.0).astype(jnp.bfloat16)
        parts = dot(weights, chosen)
        part = parts[0:32] + parts[32:64] + parts[64:96]
        high, low = split(part, 2)
        mat[0, kk * 32 : (kk + 1) * 32, :] = high
        mat[1, kk * 32 : (kk + 1) * 32, :] = low

    lane = iota((8, LANES), 1)
    sub = iota((8, LANES), 0)
    lane_group = lane >> 5
    target = 4 * sub + lane_group
    angle = jnp.zeros((8, LANES), jnp.float32)
    for t in range(LAT_BLOCK):
        angle = jnp.where(target == t, lat_ang[0, 0, 0, t], angle)
    for t in range(LON_BLOCK):
        u, v = (5, t + 1) if t < 3 else (6, t - 3)
        angle = jnp.where(target == 4 * u + v, lon_ang[0, 0, 0, t], angle)
    cos_angle = jnp.cos(angle)
    sin_angle = jnp.sin(angle)

    def export(s, x):
        columns = []
        for f in range(FIELDS):
            columns.append(x[f, 1 : GROUPS + 1, TOP : TOP + CLAT, :].reshape(GROUPS * CLAT, LANES))
        high, low = split(jnp.concatenate(columns, axis=1), 2)
        total = dot(mat[0], high) + dot(mat[0], low) + dot(mat[1], high)
        blocks = []
        for f in range(FIELDS):
            piece = total[:, f * LANES : (f + 1) * LANES]
            result = None
            for shift in range(4):
                mixed = None
                for kk in range(4):
                    v = (kk + shift) % 4
                    part = piece[kk * 32 + v * 8 : kk * 32 + v * 8 + 8, :]
                    mixed = part if mixed is None else jnp.where(lane_group == kk, part, mixed)
                if shift:
                    mixed = pltpu.roll(mixed, 32 * shift, 1)
                result = mixed if result is None else result + mixed
            blocks.append(result)
        east = cos_angle * blocks[1] + sin_angle * blocks[2]
        north = cos_angle * blocks[2] - sin_angle * blocks[1]
        blocks[1], blocks[2] = east, north
        for f in range(FIELDS):
            zbuf[s, SPAN * f : SPAN * f + SPAN, :] = blocks[f][0:SPAN]
            wbuf[s, 0, f : f + 1, :] = blocks[f][5:6]
            wbuf[s, 1, f : f + 1, :] = blocks[f][6:7]

    def rim_copies(s):
        lat_dst = rl.at[pl.ds((s * n_lat + a) * BLOCK_ROWS, BLOCK_ROWS), :]
        lon_dst = rw.at[pl.ds((s * n_lon + b) * 8, 8), :]
        ends = (
            (zbuf.at[s], lat_dst, (q, 0, b), 0),
            (zbuf.at[s], lat_dst, (q, n_lat - 1, b), 0),
            (wbuf.at[s, 0], lon_dst, (q, a, 0), 1),
            (wbuf.at[s, 1], lon_dst, (q, a, n_lon - 1), 1),
        )
        return [
            pltpu.make_async_remote_copy(
                src_ref=src,
                dst_ref=dst,
                send_sem=rim_send.at[s, i],
                recv_sem=rim_recv.at[s, kind],
                device_id=device,
                device_id_type=MESH,
            )
            for i, (src, dst, device, kind) in enumerate(ends)
        ]

    def row_copy(s, x, h):
        there = jnp.where(h == 0, jnp.logical_not(low_a), jnp.logical_not(high_a))
        return there, pltpu.make_async_remote_copy(
            src_ref=x.at[:, inner, pl.ds(TOP + (CLAT - 3) * h, 3), :],
            dst_ref=x.at[:, inner, pl.ds(TOP + CLAT - (CLAT + 3) * h, 3), :],
            send_sem=halo_send.at[s, 0, h],
            recv_sem=halo_recv.at[s, 0, h],
            device_id=(p, a + 2 * h - 1, b),
            device_id_type=MESH,
        )

    def col_copies(s, x, h):
        band = pl.ds(pl.multiple_of(TOP + 8 * h, 8), 8)
        ends = ((1, GROUPS + 1), (GROUPS, 0))
        return [
            (
                neighbours[2 + i][0],
                pltpu.make_async_remote_copy(
                    src_ref=x.at[:, src, band, :],
                    dst_ref=x.at[:, dst, band, :],
                    send_sem=halo_send.at[s, 1 + i, h],
                    recv_sem=halo_recv.at[s, 1 + i, h],
                    device_id=neighbours[2 + i][1],
                    device_id_type=MESH,
                ),
            )
            for i, (src, dst) in enumerate(ends)
        ]

    def send_half(s, x, h):
        for there, copy in [row_copy(s, x, h)] + col_copies(s, x, h):

            @pl.when(there)
            def _():
                copy.start()

    pltpu.make_async_copy(
        x1.at[:, inner, pl.ds(TOP, CLAT), :], x1.at[:, inner, pl.ds(TOP, CLAT), :], local.at[9]
    ).wait()
    export(0, x1)

    count = 4
    for there, _ in neighbours:
        count = count + jnp.where(there, 1, 0)
    pl.semaphore_wait(barrier, count)

    for copy in rim_copies(0):
        copy.start()
    for h in range(2):
        send_half(0, x1, h)

    for copy in small[6:]:
        copy.wait()
    total_rows = CLAT * n_lat
    for h in range(2):
        row = (a * CLAT + 8 * h + sub).astype(jnp.float32)
        cosine = jnp.cos((row + 0.5 - 0.5 * total_rows) * (0.5 * math.pi / total_rows))
        metric[h, 0] = 1.0 / (60.0 * cosine)
        metric[h, 1] = 1.0 / (cosine * cosine)

    k_lat = (
        4 * (iota((32, n_lat), 0) & 7)
        + (iota((32, n_lat), 0) >> 3)
        + jnp.where(low_a, 0, n_lat // 2)
    )
    choose_lat = jnp.where(lat_pair[p] == k_lat, 1.0, 0.0).astype(jnp.bfloat16)
    choose_lon = jnp.where(lon_pair[p] == iota((CLAT, n_lon), 0), 1.0, 0.0).astype(jnp.bfloat16)

    def place_lat(s, x, first_row):
        half = lane < 64
        for f in range(FIELDS):
            got = jnp.concatenate(
                [
                    rl[pl.ds(s * n_lat * BLOCK_ROWS + SPAN * f + u, n_lat, stride=BLOCK_ROWS), :]
                    for u in range(SPAN)
                ],
                axis=1,
            )
            placed = None
            for piece in split(got, 3):
                term = dot(choose_lat, piece)
                placed = term if placed is None else placed + term
            for c in range(2):
                plain = [placed[16 * c : 16 * c + 8, u * LANES : (u + 1) * LANES] for u in range(SPAN)]
                moved = [
                    pltpu.roll(placed[16 * c + 8 : 16 * c + 16, u * LANES : (u + 1) * LANES], 64, 1)
                    for u in range(SPAN)
                ]
                tiles = plain[:4] + [jnp.where(half, plain[4], moved[0])]
                tiles += [jnp.where(half, moved[u], moved[u + 1]) for u in range(4)]
                for g, value in enumerate(tiles):
                    x[f, 1 + 9 * c + g, first_row : first_row + 3, :] = value[0:3]

    def place_lon(s, x, group):
        got = jnp.concatenate(
            [rw[pl.ds(s * n_lon * 8 + f, n_lon, stride=8), :] for f in range(FIELDS)], axis=1
        )
        placed = None
        for piece in split(got, 3):
            term = dot(choose_lon, piece)
            placed = term if placed is None else placed + term
        for f in range(FIELDS):
            x[f, group, TOP : TOP + CLAT, :] = placed[:, f * LANES : (f + 1) * LANES]

    def wait_rows(s, x, h):
        there = jnp.where(h == 0, jnp.logical_not(low_a), jnp.logical_not(high_a))

        @pl.when(there)
        def _():
            row_copy(s, x, 1 - h)[1].wait_recv()

        @pl.when(jnp.logical_not(there))
        def _():
            got = rl.at[pl.ds(s * n_lat * BLOCK_ROWS, n_lat * BLOCK_ROWS), :]
            pltpu.make_async_copy(got, got, rim_recv.at[s, 0]).wait()

        @pl.when(jnp.logical_and(h == 0, low_a))
        def _():
            place_lat(s, x, TOP - 3)

        @pl.when(jnp.logical_and(h == 1, high_a))
        def _():
            place_lat(s, x, TOP + CLAT)

    def wait_cols(s, x):
        for h in range(2):
            (west, to_west), (east, to_east) = col_copies(s, x, h)

            @pl.when(west)
            def _():
                to_east.wait_recv()

            @pl.when(east)
            def _():
                to_west.wait_recv()

        @pl.when(lon_edge)
        def _():
            got = rw.at[pl.ds(s * n_lon * 8, n_lon * 8), :]
            pltpu.make_async_copy(got, got, rim_recv.at[s, 1]).wait()

        @pl.when(low_b)
        def _():
            place_lon(s, x, 0)

        @pl.when(high_b)
        def _():
            place_lon(s, x, GROUPS + 1)

    not_last = (lane & (LEV - 1)) != LEV - 1
    not_first = (lane & (LEV - 1)) != 0

    def derivatives(x, f, g, r):
        def row(o):
            return x[f, g, pl.ds(r + o, 8), :]

        here = row(0)
        west, east = x[f, g - 1, pl.ds(r, 8), :], x[f, g + 1, pl.ds(r, 8), :]
        up1, down1 = row(1), row(-1)
        lat = (
            0.75 * (up1 - down1) - 0.15 * (row(2) - row(-2)) + (1.0 / 60.0) * (row(3) - row(-3))
        )
        plus1 = pltpu.roll(jnp.where(lane < 32, east, here), 96, 1)
        minus1 = pltpu.roll(jnp.where(lane >= 96, west, here), 32, 1)
        two = pltpu.roll(jnp.where(lane < 64, east - here, here - west), 64, 1)
        plus3 = pltpu.roll(jnp.where(lane < 96, east, here), 32, 1)
        minus3 = pltpu.roll(jnp.where(lane >= 32, west, here), 96, 1)
        lon = 45.0 * (plus1 - minus1) - 9.0 * two + (plus3 - minus3)
        upper = jnp.where(not_last, pltpu.roll(here, LANES - 1, 1), 0.0)
        lower = jnp.where(not_first, pltpu.roll(here, 1, 1), 0.0)
        return here, lat, lon, upper - lower, up1 + down1, plus1 + minus1

    def group_rates(x, g, h, store):
        r = pl.multiple_of(TOP + 8 * h, 8)
        begin = pl.multiple_of((g - 1) * LANES, LANES)
        inv_lon, inv_sq = metric[h, 0], metric[h, 1]
        centre = 2.0 + 2.0 * inv_sq
        u = x[1, g, pl.ds(r, 8), :] * inv_lon
        v = x[2, g, pl.ds(r, 8), :]
        w = x[3, g, pl.ds(r, 8), :] * 0.5
        rho = x[0, g, pl.ds(r, 8), :]
        nu = visc[0, pl.ds(pl.multiple_of(8 * h, 8), 8), pl.ds(begin, LANES)]

        def plain(f):
            here, lat, lon, lev, rows_sum, cols_sum = derivatives(x, f, g, r)
            lap = rows_sum + cols_sum * inv_sq - centre * here
            return here, lat, lon, lev, nu * lap - (u * lon + v * lat + w * lev)

        e, e_lat, e_lon, e_lev, e_rate = plain(4)
        here, _, lon, _, rate = plain(1)
        div = lon * inv_lon
        store(1, g, h, begin, here, rate - KAPPA_PRESS * (e_lon * inv_lon))
        here, lat, _, _, rate = plain(2)
        div = div + lat
        store(2, g, h, begin, here, rate - KAPPA_PRESS * e_lat)
        here, _, _, lev, rate = plain(3)
        div = div + 0.5 * lev
        store(3, g, h, begin, here, rate - (0.5 * KAPPA_PRESS) * e_lev - rho)
        here, _, _, _, rate = plain(0)
        store(0, g, h, begin, here, rate - div)
        store(4, g, h, begin, e, e_rate - GAMMA_HEAT * div)

    def section(s, x, store):
        first_half = jnp.where(low_a, 1, 0)

        def block(i, carry):
            second = jnp.where(lat_edge, i // 2, i % 2)
            cols_part = jnp.where(lat_edge, i % 2, i // 2)
            h = jnp.where(second == 0, first_half, 1 - first_half)

            @pl.when(cols_part == 0)
            def _():
                wait_rows(s, x, h)

            @pl.when(jnp.logical_and(cols_part == 1, second == 0))
            def _():
                wait_cols(s, x)

            def step(k, inside):
                for one in range(2):
                    g = jnp.where(cols_part == 0, 2 + 2 * k + one, 1 + (GROUPS - 1) * one)
                    group_rates(x, g, h, store)
                return inside

            lax.fori_loop(0, jnp.where(cols_part == 0, (GROUPS - 2) // 2, 1), step, 0)
            if s == 0:

                @pl.when(cols_part == 1)
                def _():
                    send_half(1, x2, h)

            return carry

        lax.fori_loop(0, 4, block, 0)

    def store_first(f, g, h, begin, here, rate):
        x2[f, g, pl.ds(pl.multiple_of(TOP + 8 * h, 8), 8), :] = here + TIME_STEP * rate

    def store_second(f, g, h, begin, here, rate):
        before = x1[f, g, pl.ds(pl.multiple_of(TOP + 8 * h, 8), 8), :]
        out[0, f, pl.ds(pl.multiple_of(8 * h, 8), 8), pl.ds(begin, LANES)] = 0.5 * (
            before + here + TIME_STEP * rate
        )

    section(0, x1, store_first)
    export(1, x2)
    for copy in rim_copies(1):
        copy.start()
    section(1, x2, store_second)

    for s, x in enumerate((x1, x2)):
        for copy in rim_copies(s):
            copy.wait_send()
        for h in range(2):
            for there, copy in [row_copy(s, x, h)] + col_copies(s, x, h):

                @pl.when(there)
                def _():
                    copy.wait_send()


def on_device(*operands):
    n_lat = lax.axis_size("lat")
    n_lon = lax.axis_size("lon")
    operands = list(operands)
    operands[2] = operands[2].reshape(LAT_BLOCK, 1, LANES)
    operands[3] = operands[3].reshape(LON_BLOCK, 1, LANES)

    def body(*refs):
        kernel(n_lat, n_lon, *refs)

    def vmem(*shape):
        return pltpu.VMEM(shape, jnp.float32)

    return pl.pallas_call(
        body,
        out_shape=jax.ShapeDtypeStruct(operands[0].shape, jnp.float32),
        in_specs=[pl.BlockSpec(memory_space=pltpu.HBM)] * 10,
        out_specs=pl.BlockSpec(memory_space=pltpu.VMEM),
        scratch_shapes=[
            vmem(FIELDS, GROUPS + 2, 32, LANES),
            vmem(FIELDS, GROUPS + 2, 32, LANES),
            vmem(1, CLAT, GROUPS * LANES),
            vmem(LAT_BLOCK, 1, LANES),
            vmem(LON_BLOCK, 1, LANES),
            pltpu.SMEM((1, 1, 1, LAT_BLOCK), jnp.float32),
            pltpu.SMEM((1, 1, 1, LON_BLOCK), jnp.float32),
            pltpu.SMEM((1, 1, 1, 2), jnp.int32),
            pltpu.SMEM((1, 1, 1, 2), jnp.int32),
            pltpu.VMEM((2, 1, n_lat), jnp.int32),
            pltpu.VMEM((2, 1, n_lon), jnp.int32),
            vmem(32, 2 * LANES),
            pltpu.VMEM((2, LANES, GROUPS * CLAT), jnp.bfloat16),
            vmem(2, 2, 8, LANES),
            vmem(2, BLOCK_ROWS, LANES),
            vmem(2, 2, 8, LANES),
            vmem(2 * n_lat * BLOCK_ROWS, LANES),
            vmem(2 * n_lon * 8, LANES),
            pltpu.SemaphoreType.DMA((10,)),
            pltpu.SemaphoreType.DMA((2, 3, 2)),
            pltpu.SemaphoreType.DMA((2, 3, 2)),
            pltpu.SemaphoreType.DMA((2, 4)),
            pltpu.SemaphoreType.DMA((2, 2)),
        ],
        compiler_params=pltpu.CompilerParams(
            collective_id=0, has_side_effects=True, vmem_limit_bytes=56 * 1024 * 1024
        ),
    )(*operands)


def solution(mesh):
    in_specs = (
        P("yy", None, "lat", "lon"),
        P("yy", "lat", "lon"),
        P("yy", "lat", "lon", None, None),
        P("yy", "lat", "lon", None, None),
        P("yy", "lat", "lon", None),
        P("yy", "lat", "lon", None),
        P("yy", "lat", "lon", None),
        P("yy", "lat", "lon", None),
        P(None, "lon", None),
        P(None, "lat", None),
    )
    out_specs = P("yy", None, "lat", "lon")
    return jax.shard_map(
        on_device, mesh=mesh, in_specs=in_specs, out_specs=out_specs, check_vma=False
    )
```

time: 48.7 us -> 43.3 us (0.89)
  Pallas kernels: 44 us -> 41 us
  local copies, waits for them, and re-layouts: 4.36 us -> 2.03 us
    pallas_call x1, Pallas kernels: 44 us -> 41 us  [on_device(): pl.pallas_call(body, out_shape=jax.ShapeDtypeStruct(operands[0].shape, jn...]
    unnamed x19 -> x1, local copies, waits for them, and re-layouts: 4.36 us -> 2.03 us
where the time goes in v2:
time: 43.3 us; the launch traced here: 43.1 us
  Pallas kernels  41 us (95%)
  local copies, waits for them, and re-layouts  2.03 us (5%)
    pallas_call x1, Pallas kernels, on_device(): pl.pallas_call(body, out_shape=jax.ShapeDtypeStruct(operands[0].shape, jn...  41 us
    unnamed x1, local copies, waits for them, and re-layouts  2.03 us

profile of v2, /device:TPU:1, one launch (start us, length us, event | category | flops | bytes accessed | tf_op | source)
XLA Modules:
  0.0 43.1 jit_solution(11143907584806044634)
XLA Ops:
  0.0 41.0 %shard_map.100 = f32[1,5,16,2304]{3,2,1,0:T(8,128)} custom-call(f32[1,5,16,2304]{3,2,1,0:T(8,128)} %refs_0_.1, f32[1,16,2304]{2,1,0:T(8,128)} %refs_1_.1, f32[18,1,128]{2,1,0:T(1,128)} %bitcast.2, f32[6,1,128]{2,1,0:T(1,128)} %bitcast.3, f32[1,1,1,18]{3,2,1,0:T(1,128)} %refs_4_.1, f32[1,1,1,6]{3,2,1,0:T(1,128)} %refs_5_.1, s32[1,1,1,2]{3,2,1,0:T(1,128)} %refs_6_.1, ...), custom_call_target="tpu_custom_call" | custom-call | tf_op jit(solution)/shard_map/pallas_call | solution.py:514
  41.0 2.0 %copy.12 = f32[1,5,16,2304]{3,2,1,0:T(8,128)} copy(f32[1,5,16,2304]{3,2,1,0:T(8,128)} %shard_map.100) | data formatting | bytes 1474560

commit v3 on v2

--- a/solution.py
+++ b/solution.py
@@ -97,6 +97,29 @@
         (jnp.logical_not(high_b), (p, a, b + 1)),
     )
 
+    barrier = pltpu.get_barrier_semaphore()
+    for there, device in neighbours:
+
+        @pl.when(there)
+        def _():
+            pl.semaphore_signal(barrier, inc=1, device_id=device, device_id_type=MESH)
+
+    @pl.when(lat_edge)
+    def _():
+        def one(i, carry):
+            pl.semaphore_signal(barrier, inc=1, device_id=(q, i, b), device_id_type=MESH)
+            return carry
+
+        lax.fori_loop(0, n_lat, one, 0)
+
+    @pl.when(lon_edge)
+    def _():
+        def one(i, carry):
+            pl.semaphore_signal(barrier, inc=1, device_id=(q, a, i), device_id_type=MESH)
+            return carry
+
+        lax.fori_loop(0, n_lon, one, 0)
+
     small = [
         pltpu.make_async_copy(src, dst, local.at[i])
         for i, (src, dst) in enumerate(
@@ -125,29 +148,6 @@
     for copy in small[6:]:
         copy.start()
 
-    barrier = pltpu.get_barrier_semaphore()
-    for there, device in neighbours:
-
-        @pl.when(there)
-        def _():
-            pl.semaphore_signal(barrier, inc=1, device_id=device, device_id_type=MESH)
-
-    @pl.when(lat_edge)
-    def _():
-        def one(i, carry):
-            pl.semaphore_signal(barrier, inc=1, device_id=(q, i, b), device_id_type=MESH)
-            return carry
-
-        lax.fori_loop(0, n_lat, one, 0)
-
-    @pl.when(lon_edge)
-    def _():
-        def one(i, carry):
-            pl.semaphore_signal(barrier, inc=1, device_id=(q, a, i), device_id_type=MESH)
-            return carry
-
-        lax.fori_loop(0, n_lon, one, 0)
-
     wp[...] = jnp.zeros_like(wp)
     for copy in small[:6]:
         copy.wait()
@@ -504,6 +504,7 @@
     operands = list(operands)
     operands[2] = operands[2].reshape(LAT_BLOCK, 1, LANES)
     operands[3] = operands[3].reshape(LON_BLOCK, 1, LANES)
+    operands = [pltpu.with_memory_space_constraint(x, pltpu.HBM) for x in operands]
 
     def body(*refs):
         kernel(n_lat, n_lon, *refs)
@@ -542,7 +543,7 @@
             pltpu.SemaphoreType.DMA((2, 2)),
         ],
         compiler_params=pltpu.CompilerParams(
-            collective_id=0, has_side_effects=True, vmem_limit_bytes=56 * 1024 * 1024
+            collective_id=0, has_side_effects=True, vmem_limit_bytes=40 * 1024 * 1024
         ),
     )(*operands)
 

time: 43.3 us -> 41.1 us (0.949)
  local copies, waits for them, and re-layouts: 2.03 us -> 0.87 us
  Pallas kernels: 41 us -> 40.1 us
    unnamed x1, local copies, waits for them, and re-layouts: 2.03 us -> 0.87 us
    pallas_call x1, Pallas kernels: 41 us -> 40.1 us  [on_device(): pl.pallas_call(body, out_shape=jax.ShapeDtypeStruct(operands[0].shape, jn...]
where the time goes in v3:
time: 41.1 us; the launch traced here: 41 us
  Pallas kernels  40.1 us (98%)
  local copies, waits for them, and re-layouts  0.87 us (2%)
    pallas_call x1, Pallas kernels, on_device(): pl.pallas_call(body, out_shape=jax.ShapeDtypeStruct(operands[0].shape, jn...  40.1 us
    unnamed x1, local copies, waits for them, and re-layouts  0.87 us

profile of v3, /device:TPU:1, one launch (start us, length us, event | category | flops | bytes accessed | tf_op | source)
XLA Modules:
  0.0 41.0 jit_solution(4852819684148790669)
XLA Ops:
  0.0 40.1 %shard_map.100 = f32[1,5,16,2304]{3,2,1,0:T(8,128)S(1)} custom-call(f32[1,5,16,2304]{3,2,1,0:T(8,128)} %refs_0_.1, f32[1,16,2304]{2,1,0:T(8,128)} %refs_1_.1, f32[18,1,128]{2,1,0:T(1,128)} %bitcast.2, f32[6,1,128]{2,1,0:T(1,128)} %bitcast.3, f32[1,1,1,18]{3,2,1,0:T(1,128)} %refs_4_.1, f32[1,1,1,6]{3,2,1,0:T(1,128)} %refs_5_.1, s32[1,1,1,2]{3,2,1,0:T(1,128)} %refs_6_.1, ...), custom_call_target="tpu_custom_call" | custom-call | tf_op jit(solution)/shard_map/pallas_call | solution.py:515
  40.1 0.9 %copy.12 = f32[1,5,16,2304]{3,2,1,0:T(8,128)} copy(f32[1,5,16,2304]{3,2,1,0:T(8,128)S(1)} %shard_map.100) | data formatting | bytes 1474560

commit v4 on v3

--- a/solution.py
+++ b/solution.py
@@ -60,6 +60,7 @@
     out,
     x1,
     x2,
+    hz,
     visc,
     lat_w,
     lon_w,
@@ -241,7 +242,7 @@
         there = jnp.where(h == 0, jnp.logical_not(low_a), jnp.logical_not(high_a))
         return there, pltpu.make_async_remote_copy(
             src_ref=x.at[:, inner, pl.ds(TOP + (CLAT - 3) * h, 3), :],
-            dst_ref=x.at[:, inner, pl.ds(TOP + CLAT - (CLAT + 3) * h, 3), :],
+            dst_ref=hz.at[s, 1 - h, :, :, pl.ds(8 - 3 * h, 3), :],
             send_sem=halo_send.at[s, 0, h],
             recv_sem=halo_recv.at[s, 0, h],
             device_id=(p, a + 2 * h - 1, b),
@@ -288,6 +289,19 @@
     for h in range(2):
         send_half(0, x1, h)
 
+    none = jnp.zeros((8, LANES), jnp.float32)
+
+    def clear(g, carry):
+        for f in range(FIELDS):
+            for s, x in enumerate((x1, x2)):
+                x[f, g + 1, TOP - 8 : TOP, :] = none
+                x[f, g + 1, TOP + CLAT : TOP + CLAT + 8, :] = none
+                hz[s, 0, f, g, 8:16, :] = none
+                hz[s, 1, f, g, 0:8, :] = none
+        return carry
+
+    lax.fori_loop(0, GROUPS, clear, 0)
+
     for copy in small[6:]:
         copy.wait()
     total_rows = CLAT * n_lat
@@ -305,7 +319,7 @@
     choose_lat = jnp.where(lat_pair[p] == k_lat, 1.0, 0.0).astype(jnp.bfloat16)
     choose_lon = jnp.where(lon_pair[p] == iota((CLAT, n_lon), 0), 1.0, 0.0).astype(jnp.bfloat16)
 
-    def place_lat(s, x, first_row):
+    def place_lat(s, side, first_row):
         half = lane < 64
         for f in range(FIELDS):
             got = jnp.concatenate(
@@ -328,7 +342,7 @@
                 tiles = plain[:4] + [jnp.where(half, plain[4], moved[0])]
                 tiles += [jnp.where(half, moved[u], moved[u + 1]) for u in range(4)]
                 for g, value in enumerate(tiles):
-                    x[f, 1 + 9 * c + g, first_row : first_row + 3, :] = value[0:3]
+                    hz[s, side, f, 9 * c + g, first_row : first_row + 3, :] = value[0:3]
 
     def place_lon(s, x, group):
         got = jnp.concatenate(
@@ -341,12 +355,12 @@
         for f in range(FIELDS):
             x[f, group, TOP : TOP + CLAT, :] = placed[:, f * LANES : (f + 1) * LANES]
 
-    def wait_rows(s, x, h):
+    def wait_rows(s, h):
         there = jnp.where(h == 0, jnp.logical_not(low_a), jnp.logical_not(high_a))
 
         @pl.when(there)
         def _():
-            row_copy(s, x, 1 - h)[1].wait_recv()
+            row_copy(s, x1, 1 - h)[1].wait_recv()
 
         @pl.when(jnp.logical_not(there))
         def _():
@@ -355,11 +369,11 @@
 
         @pl.when(jnp.logical_and(h == 0, low_a))
         def _():
-            place_lat(s, x, TOP - 3)
+            place_lat(s, 0, 5)
 
         @pl.when(jnp.logical_and(h == 1, high_a))
         def _():
-            place_lat(s, x, TOP + CLAT)
+            place_lat(s, 1, 8)
 
     def wait_cols(s, x):
         for h in range(2):
@@ -439,38 +453,62 @@
         store(0, g, h, begin, here, rate - div)
         store(4, g, h, begin, e, e_rate - GAMMA_HEAT * div)
 
-    def section(s, x, store):
-        first_half = jnp.where(low_a, 1, 0)
-
+    def correct(s, x, h, add):
+        r = pl.multiple_of(TOP + 8 * h, 8)
+        sign = jnp.where(h == 0, -1.0, 1.0)
+
+        def step(k, carry):
+            for one in range(2):
+                g = 1 + 2 * k + one
+                begin = pl.multiple_of((g - 1) * LANES, LANES)
+                v = x[2, g, pl.ds(r, 8), :]
+                nu = visc[0, pl.ds(pl.multiple_of(8 * h, 8), 8), pl.ds(begin, LANES)]
+
+                def share(f):
+                    near, middle, far = (
+                        hz[s, h, f, g - 1, pl.ds(jnp.where(h == 0, 8 - o, o), 8), :]
+                        for o in (1, 2, 3)
+                    )
+                    lat = sign * (0.75 * near - 0.15 * middle + (1.0 / 60.0) * far)
+                    return lat, nu * near - v * lat
+
+                e_lat, e_rate = share(4)
+                v_lat, v_rate = share(2)
+                add(2, g, h, begin, v_rate - KAPPA_PRESS * e_lat)
+                add(4, g, h, begin, e_rate - GAMMA_HEAT * v_lat)
+                add(0, g, h, begin, share(0)[1] - v_lat)
+                add(1, g, h, begin, share(1)[1])
+                add(3, g, h, begin, share(3)[1])
+            return carry
+
+        lax.fori_loop(0, GROUPS // 2, step, 0)
+
+    def section(s, x, store, add):
         def block(i, carry):
-            second = jnp.where(lat_edge, i // 2, i % 2)
-            cols_part = jnp.where(lat_edge, i % 2, i // 2)
-            h = jnp.where(second == 0, first_half, 1 - first_half)
-
-            @pl.when(cols_part == 0)
-            def _():
-                wait_rows(s, x, h)
-
-            @pl.when(jnp.logical_and(cols_part == 1, second == 0))
+            @pl.when(i == 1)
             def _():
                 wait_cols(s, x)
 
             def step(k, inside):
                 for one in range(2):
-                    g = jnp.where(cols_part == 0, 2 + 2 * k + one, 1 + (GROUPS - 1) * one)
-                    group_rates(x, g, h, store)
+                    g = jnp.where(i == 0, 2 + 2 * (k // 2) + one, 1 + (GROUPS - 1) * one)
+                    group_rates(x, g, k % 2, store)
                 return inside
 
-            lax.fori_loop(0, jnp.where(cols_part == 0, (GROUPS - 2) // 2, 1), step, 0)
+            lax.fori_loop(0, jnp.where(i == 0, GROUPS - 2, 2), step, 0)
+            return carry
+
+        lax.fori_loop(0, 2, block, 0)
+
+        def side(i, carry):
+            h = jnp.where(low_a, 1 - i, i)
+            wait_rows(s, h)
+            correct(s, x, h, add)
             if s == 0:
-
-                @pl.when(cols_part == 1)
-                def _():
-                    send_half(1, x2, h)
-
+                send_half(1, x2, h)
             return carry
 
-        lax.fori_loop(0, 4, block, 0)
+        lax.fori_loop(0, 2, side, 0)
 
     def store_first(f, g, h, begin, here, rate):
         x2[f, g, pl.ds(pl.multiple_of(TOP + 8 * h, 8), 8), :] = here + TIME_STEP * rate
@@ -481,11 +519,19 @@
             before + here + TIME_STEP * rate
         )
 
-    section(0, x1, store_first)
+    def add_first(f, g, h, begin, rate):
+        x2[f, g, pl.ds(pl.multiple_of(TOP + 8 * h, 8), 8), :] += TIME_STEP * rate
+
+    def add_second(f, g, h, begin, rate):
+        out[0, f, pl.ds(pl.multiple_of(8 * h, 8), 8), pl.ds(begin, LANES)] += (
+            0.5 * TIME_STEP * rate
+        )
+
+    section(0, x1, store_first, add_first)
     export(1, x2)
     for copy in rim_copies(1):
         copy.start()
-    section(1, x2, store_second)
+    section(1, x2, store_second, add_second)
 
     for s, x in enumerate((x1, x2)):
         for copy in rim_copies(s):
@@ -520,6 +566,7 @@
         scratch_shapes=[
             vmem(FIELDS, GROUPS + 2, 32, LANES),
             vmem(FIELDS, GROUPS + 2, 32, LANES),
+            vmem(2, 2, FIELDS, GROUPS, 16, LANES),
             vmem(1, CLAT, GROUPS * LANES),
             vmem(LAT_BLOCK, 1, LANES),
             vmem(LON_BLOCK, 1, LANES),

time: 41.1 us -> 38.5 us (0.937)
  Pallas kernels: 40.1 us -> 37.4 us
    pallas_call x1, Pallas kernels: 40.1 us -> 37.4 us  [on_device(): pl.pallas_call(body, out_shape=jax.ShapeDtypeStruct(operands[0].shape, jn...]
where the time goes in v4:
time: 38.5 us; the launch traced here: 38.3 us
  Pallas kernels  37.4 us (97%)
  local copies, waits for them, and re-layouts  0.87 us (2%)
    pallas_call x1, Pallas kernels, on_device(): pl.pallas_call(body, out_shape=jax.ShapeDtypeStruct(operands[0].shape, jn...  37.4 us
    unnamed x1, local copies, waits for them, and re-layouts  0.87 us

profile of v4, /device:TPU:1, one launch (start us, length us, event | category | flops | bytes accessed | tf_op | source)
XLA Modules:
  0.0 38.3 jit_solution(2647525405977830135)
XLA Ops:
  0.0 37.4 %shard_map.100 = f32[1,5,16,2304]{3,2,1,0:T(8,128)S(1)} custom-call(f32[1,5,16,2304]{3,2,1,0:T(8,128)} %refs_0_.1, f32[1,16,2304]{2,1,0:T(8,128)} %refs_1_.1, f32[18,1,128]{2,1,0:T(1,128)} %bitcast.2, f32[6,1,128]{2,1,0:T(1,128)} %bitcast.3, f32[1,1,1,18]{3,2,1,0:T(1,128)} %refs_4_.1, f32[1,1,1,6]{3,2,1,0:T(1,128)} %refs_5_.1, s32[1,1,1,2]{3,2,1,0:T(1,128)} %refs_6_.1, ...), custom_call_target="tpu_custom_call" | custom-call | tf_op jit(solution)/shard_map/pallas_call | solution.py:561
  37.4 0.9 %copy.12 = f32[1,5,16,2304]{3,2,1,0:T(8,128)} copy(f32[1,5,16,2304]{3,2,1,0:T(8,128)S(1)} %shard_map.100) | data formatting | bytes 1474560

commit v5 on v4

--- a/solution.py
+++ b/solution.py
@@ -17,7 +17,8 @@
 LAT_BLOCK = 18
 LON_BLOCK = 6
 SPAN = 5
-BLOCK_ROWS = 32
+BLOCK_ROWS = 23
+WIDE_ROWS = 5
 TOP = 8
 
 TIME_STEP = 0.2
@@ -107,11 +108,18 @@
 
     @pl.when(lat_edge)
     def _():
-        def one(i, carry):
-            pl.semaphore_signal(barrier, inc=1, device_id=(q, i, b), device_id_type=MESH)
+        ring = n_lat // 2
+
+        def one(k, carry):
+            away = ring // 2 + jnp.where(k % 2 == 1, -((k + 1) // 2), k // 2)
+            for part in range(2):
+                there = part * ring + lax.rem(a + away, ring)
+                pl.semaphore_signal(
+                    barrier, inc=1, device_id=(q, there, b), device_id_type=MESH
+                )
             return carry
 
-        lax.fori_loop(0, n_lat, one, 0)
+        lax.fori_loop(0, ring, one, 0)
 
     @pl.when(lon_edge)
     def _():
@@ -213,13 +221,20 @@
         north = cos_angle * blocks[2] - sin_angle * blocks[1]
         blocks[1], blocks[2] = east, north
         for f in range(FIELDS):
-            zbuf[s, SPAN * f : SPAN * f + SPAN, :] = blocks[f][0:SPAN]
+            zbuf[s, 4 * f : 4 * f + 4, :] = blocks[f][0:4]
+            last = blocks[f][4:5]
+            if f % 2 == 0 and f + 1 < FIELDS:
+                last = jnp.where(
+                    lane[0:1] < 64, last, pltpu.roll(blocks[f + 1], 64, 1)[4:5]
+                )
+            if f % 2 == 0:
+                zbuf[s, 4 * FIELDS + f // 2 : 4 * FIELDS + f // 2 + 1, :] = last
             wbuf[s, 0, f : f + 1, :] = blocks[f][5:6]
             wbuf[s, 1, f : f + 1, :] = blocks[f][6:7]
 
     def rim_copies(s):
         lat_dst = rl.at[pl.ds((s * n_lat + a) * BLOCK_ROWS, BLOCK_ROWS), :]
-        lon_dst = rw.at[pl.ds((s * n_lon + b) * 8, 8), :]
+        lon_dst = rw.at[pl.ds((s * n_lon + b) * WIDE_ROWS, WIDE_ROWS), :]
         ends = (
             (zbuf.at[s], lat_dst, (q, 0, b), 0),
             (zbuf.at[s], lat_dst, (q, n_lat - 1, b), 0),
@@ -284,7 +299,7 @@
         count = count + jnp.where(there, 1, 0)
     pl.semaphore_wait(barrier, count)
 
-    for copy in rim_copies(0):
+    for copy in rim_copies(0)[::-1]:
         copy.start()
     for h in range(2):
         send_half(0, x1, h)
@@ -319,13 +334,16 @@
     choose_lat = jnp.where(lat_pair[p] == k_lat, 1.0, 0.0).astype(jnp.bfloat16)
     choose_lon = jnp.where(lon_pair[p] == iota((CLAT, n_lon), 0), 1.0, 0.0).astype(jnp.bfloat16)
 
+    def moved_last(placed, row):
+        return pltpu.roll(placed[row : row + 8, 4 * LANES :], 64, 1)
+
     def place_lat(s, side, first_row):
         half = lane < 64
         for f in range(FIELDS):
             got = jnp.concatenate(
                 [
-                    rl[pl.ds(s * n_lat * BLOCK_ROWS + SPAN * f + u, n_lat, stride=BLOCK_ROWS), :]
-                    for u in range(SPAN)
+                    rl[pl.ds(s * n_lat * BLOCK_ROWS + row, n_lat, stride=BLOCK_ROWS), :]
+                    for row in [4 * f + u for u in range(4)] + [4 * FIELDS + f // 2]
                 ],
                 axis=1,
             )
@@ -339,6 +357,8 @@
                     pltpu.roll(placed[16 * c + 8 : 16 * c + 16, u * LANES : (u + 1) * LANES], 64, 1)
                     for u in range(SPAN)
                 ]
+                if f % 2:
+                    plain[4], moved[4] = moved_last(placed, 16 * c), placed[16 * c + 8 : 16 * c + 16, 4 * LANES :]
                 tiles = plain[:4] + [jnp.where(half, plain[4], moved[0])]
                 tiles += [jnp.where(half, moved[u], moved[u + 1]) for u in range(4)]
                 for g, value in enumerate(tiles):
@@ -346,7 +366,7 @@
 
     def place_lon(s, x, group):
         got = jnp.concatenate(
-            [rw[pl.ds(s * n_lon * 8 + f, n_lon, stride=8), :] for f in range(FIELDS)], axis=1
+            [rw[pl.ds(s * n_lon * WIDE_ROWS + f, n_lon, stride=WIDE_ROWS), :] for f in range(FIELDS)], axis=1
         )
         placed = None
         for piece in split(got, 3):
@@ -389,7 +409,7 @@
 
         @pl.when(lon_edge)
         def _():
-            got = rw.at[pl.ds(s * n_lon * 8, n_lon * 8), :]
+            got = rw.at[pl.ds(s * n_lon * WIDE_ROWS, n_lon * WIDE_ROWS), :]
             pltpu.make_async_copy(got, got, rim_recv.at[s, 1]).wait()
 
         @pl.when(low_b)
@@ -504,8 +524,6 @@
             h = jnp.where(low_a, 1 - i, i)
             wait_rows(s, h)
             correct(s, x, h, add)
-            if s == 0:
-                send_half(1, x2, h)
             return carry
 
         lax.fori_loop(0, 2, side, 0)
@@ -529,8 +547,10 @@
 
     section(0, x1, store_first, add_first)
     export(1, x2)
-    for copy in rim_copies(1):
+    for copy in rim_copies(1)[::-1]:
         copy.start()
+    for h in range(2):
+        send_half(1, x2, h)
     section(1, x2, store_second, add_second)
 
     for s, x in enumerate((x1, x2)):
@@ -580,9 +600,9 @@
             pltpu.VMEM((2, LANES, GROUPS * CLAT), jnp.bfloat16),
             vmem(2, 2, 8, LANES),
             vmem(2, BLOCK_ROWS, LANES),
-            vmem(2, 2, 8, LANES),
+            vmem(2, 2, WIDE_ROWS, LANES),
             vmem(2 * n_lat * BLOCK_ROWS, LANES),
-            vmem(2 * n_lon * 8, LANES),
+            vmem(2 * n_lon * WIDE_ROWS, LANES),
             pltpu.SemaphoreType.DMA((10,)),
             pltpu.SemaphoreType.DMA((2, 3, 2)),
             pltpu.SemaphoreType.DMA((2, 3, 2)),

time: 38.5 us -> 37.4 us (0.971)
  Pallas kernels: 37.4 us -> 36.4 us
    pallas_call x1, Pallas kernels: 37.4 us -> 36.4 us  [on_device(): pl.pallas_call(body, out_shape=jax.ShapeDtypeStruct(operands[0].shape, jn...]
where the time goes in v5:
time: 37.4 us; the launch traced here: 37.2 us
  Pallas kernels  36.4 us (97%)
  local copies, waits for them, and re-layouts  0.87 us (2%)
    pallas_call x1, Pallas kernels, on_device(): pl.pallas_call(body, out_shape=jax.ShapeDtypeStruct(operands[0].shape, jn...  36.4 us
    unnamed x1, local copies, waits for them, and re-layouts  0.87 us

profile of v5, /device:TPU:1, one launch (start us, length us, event | category | flops | bytes accessed | tf_op | source)
XLA Modules:
  0.0 37.2 jit_solution(9758578679385486154)
XLA Ops:
  0.0 36.4 %shard_map.100 = f32[1,5,16,2304]{3,2,1,0:T(8,128)S(1)} custom-call(f32[1,5,16,2304]{3,2,1,0:T(8,128)} %refs_0_.1, f32[1,16,2304]{2,1,0:T(8,128)} %refs_1_.1, f32[18,1,128]{2,1,0:T(1,128)} %bitcast.2, f32[6,1,128]{2,1,0:T(1,128)} %bitcast.3, f32[1,1,1,18]{3,2,1,0:T(1,128)} %refs_4_.1, f32[1,1,1,6]{3,2,1,0:T(1,128)} %refs_5_.1, s32[1,1,1,2]{3,2,1,0:T(1,128)} %refs_6_.1, ...), custom_call_target="tpu_custom_call" | custom-call | tf_op jit(solution)/shard_map/pallas_call | solution.py:581
  36.4 0.9 %copy.12 = f32[1,5,16,2304]{3,2,1,0:T(8,128)} copy(f32[1,5,16,2304]{3,2,1,0:T(8,128)S(1)} %shard_map.100) | data formatting | bytes 1474560

commit v6 on v5

--- a/solution.py
+++ b/solution.py
@@ -83,6 +83,7 @@
     halo_recv,
     rim_send,
     rim_recv,
+    north_ready,
 ):
     p = lax.axis_index("yy")
     a = lax.axis_index("lat")
@@ -90,7 +91,6 @@
     q = 1 - p
     low_a, high_a = a == 0, a == n_lat - 1
     low_b, high_b = b == 0, b == n_lon - 1
-    lat_edge = jnp.logical_or(low_a, high_a)
     lon_edge = jnp.logical_or(low_b, high_b)
     neighbours = (
         (jnp.logical_not(low_a), (p, a - 1, b)),
@@ -106,20 +106,25 @@
         def _():
             pl.semaphore_signal(barrier, inc=1, device_id=device, device_id_type=MESH)
 
-    @pl.when(lat_edge)
-    def _():
-        ring = n_lat // 2
-
+    ring = n_lat // 2
+
+    def signal_sources(semaphore):
         def one(k, carry):
             away = ring // 2 + jnp.where(k % 2 == 1, -((k + 1) // 2), k // 2)
             for part in range(2):
                 there = part * ring + lax.rem(a + away, ring)
                 pl.semaphore_signal(
-                    barrier, inc=1, device_id=(q, there, b), device_id_type=MESH
+                    semaphore, inc=1, device_id=(q, there, b), device_id_type=MESH
                 )
             return carry
 
         lax.fori_loop(0, ring, one, 0)
+
+    @pl.when(low_a)
+    def _():
+        signal_sources(barrier)
+
+    pl.semaphore_signal(barrier, inc=1, device_id=(q, n_lat - 1, b), device_id_type=MESH)
 
     @pl.when(lon_edge)
     def _():
@@ -232,7 +237,7 @@
             wbuf[s, 0, f : f + 1, :] = blocks[f][5:6]
             wbuf[s, 1, f : f + 1, :] = blocks[f][6:7]
 
-    def rim_copies(s):
+    def rim_copies(s, which=(3, 2, 1, 0)):
         lat_dst = rl.at[pl.ds((s * n_lat + a) * BLOCK_ROWS, BLOCK_ROWS), :]
         lon_dst = rw.at[pl.ds((s * n_lon + b) * WIDE_ROWS, WIDE_ROWS), :]
         ends = (
@@ -250,7 +255,7 @@
                 device_id=device,
                 device_id_type=MESH,
             )
-            for i, (src, dst, device, kind) in enumerate(ends)
+            for i, (src, dst, device, kind) in [(i, ends[i]) for i in which]
         ]
 
     def row_copy(s, x, h):
@@ -294,12 +299,16 @@
     ).wait()
     export(0, x1)
 
-    count = 4
+    count = 3 + jnp.where(high_a, n_lat, 0)
     for there, _ in neighbours:
         count = count + jnp.where(there, 1, 0)
     pl.semaphore_wait(barrier, count)
 
-    for copy in rim_copies(0)[::-1]:
+    @pl.when(high_a)
+    def _():
+        signal_sources(north_ready)
+
+    for copy in rim_copies(0, (3, 2, 0)):
         copy.start()
     for h in range(2):
         send_half(0, x1, h)
@@ -507,6 +516,9 @@
         def block(i, carry):
             @pl.when(i == 1)
             def _():
+                if s == 0:
+                    pl.semaphore_wait(north_ready, 1)
+                    rim_copies(0, (1,))[0].start()
                 wait_cols(s, x)
 
             def step(k, inside):
@@ -547,7 +559,7 @@
 
     section(0, x1, store_first, add_first)
     export(1, x2)
-    for copy in rim_copies(1)[::-1]:
+    for copy in rim_copies(1):
         copy.start()
     for h in range(2):
         send_half(1, x2, h)
@@ -608,6 +620,7 @@
             pltpu.SemaphoreType.DMA((2, 3, 2)),
             pltpu.SemaphoreType.DMA((2, 4)),
             pltpu.SemaphoreType.DMA((2, 2)),
+            pltpu.SemaphoreType.REGULAR,
         ],
         compiler_params=pltpu.CompilerParams(
             collective_id=0, has_side_effects=True, vmem_limit_bytes=40 * 1024 * 1024

time: 37.4 us -> 35.2 us (0.941)
  Pallas kernels: 36.4 us -> 34.2 us
    pallas_call x1, Pallas kernels: 36.4 us -> 34.2 us  [on_device(): pl.pallas_call(body, out_shape=jax.ShapeDtypeStruct(operands[0].shape, jn...]
where the time goes in v6:
time: 35.2 us; the launch traced here: 35.1 us
  Pallas kernels  34.2 us (97%)
  local copies, waits for them, and re-layouts  0.87 us (2%)
    pallas_call x1, Pallas kernels, on_device(): pl.pallas_call(body, out_shape=jax.ShapeDtypeStruct(operands[0].shape, jn...  34.2 us
    unnamed x1, local copies, waits for them, and re-layouts  0.87 us

profile of v6, /device:TPU:1, one launch (start us, length us, event | category | flops | bytes accessed | tf_op | source)
XLA Modules:
  0.0 35.1 jit_solution(5172992601002981076)
XLA Ops:
  0.0 34.2 %shard_map.100 = f32[1,5,16,2304]{3,2,1,0:T(8,128)S(1)} custom-call(f32[1,5,16,2304]{3,2,1,0:T(8,128)} %refs_0_.1, f32[1,16,2304]{2,1,0:T(8,128)} %refs_1_.1, f32[18,1,128]{2,1,0:T(1,128)} %bitcast.2, f32[6,1,128]{2,1,0:T(1,128)} %bitcast.3, f32[1,1,1,18]{3,2,1,0:T(1,128)} %refs_4_.1, f32[1,1,1,6]{3,2,1,0:T(1,128)} %refs_5_.1, s32[1,1,1,2]{3,2,1,0:T(1,128)} %refs_6_.1, ...), custom_call_target="tpu_custom_call" | custom-call | tf_op jit(solution)/shard_map/pallas_call | solution.py:593
  34.2 0.9 %copy.12 = f32[1,5,16,2304]{3,2,1,0:T(8,128)} copy(f32[1,5,16,2304]{3,2,1,0:T(8,128)S(1)} %shard_map.100) | data formatting | bytes 1474560

commit v7 on v6

--- a/solution.py
+++ b/solution.py
@@ -162,6 +162,15 @@
     for copy in small[6:]:
         copy.start()
 
+    count = 3 + jnp.where(high_a, n_lat, 0)
+    for there, _ in neighbours:
+        count = count + jnp.where(there, 1, 0)
+
+    @pl.when(high_a)
+    def _():
+        pl.semaphore_wait(barrier, count)
+        signal_sources(north_ready)
+
     wp[...] = jnp.zeros_like(wp)
     for copy in small[:6]:
         copy.wait()
@@ -299,14 +308,9 @@
     ).wait()
     export(0, x1)
 
-    count = 3 + jnp.where(high_a, n_lat, 0)
-    for there, _ in neighbours:
-        count = count + jnp.where(there, 1, 0)
-    pl.semaphore_wait(barrier, count)
-
-    @pl.when(high_a)
+    @pl.when(jnp.logical_not(high_a))
     def _():
-        signal_sources(north_ready)
+        pl.semaphore_wait(barrier, count)
 
     for copy in rim_copies(0, (3, 2, 0)):
         copy.start()
@@ -518,7 +522,7 @@
             def _():
                 if s == 0:
                     pl.semaphore_wait(north_ready, 1)
-                    rim_copies(0, (1,))[0].start()
+                rim_copies(s, (1,))[0].start()
                 wait_cols(s, x)
 
             def step(k, inside):
@@ -559,7 +563,7 @@
 
     section(0, x1, store_first, add_first)
     export(1, x2)
-    for copy in rim_copies(1):
+    for copy in rim_copies(1, (0, 3, 2)):
         copy.start()
     for h in range(2):
         send_half(1, x2, h)

time: 35.2 us -> 35.4 us (level)
  no operation moved by 1% of the time
where the time goes in v7:
time: 35.4 us; the launch traced here: 35.2 us
  Pallas kernels  34.3 us (97%)
  local copies, waits for them, and re-layouts  0.87 us (2%)
    pallas_call x1, Pallas kernels, on_device(): pl.pallas_call(body, out_shape=jax.ShapeDtypeStruct(operands[0].shape, jn...  34.3 us
    unnamed x1, local copies, waits for them, and re-layouts  0.87 us

profile of v7, /device:TPU:1, one launch (start us, length us, event | category | flops | bytes accessed | tf_op | source)
XLA Modules:
  0.0 35.2 jit_solution(7054186868865818558)
XLA Ops:
  0.0 34.3 %shard_map.100 = f32[1,5,16,2304]{3,2,1,0:T(8,128)S(1)} custom-call(f32[1,5,16,2304]{3,2,1,0:T(8,128)} %refs_0_.1, f32[1,16,2304]{2,1,0:T(8,128)} %refs_1_.1, f32[18,1,128]{2,1,0:T(1,128)} %bitcast.2, f32[6,1,128]{2,1,0:T(1,128)} %bitcast.3, f32[1,1,1,18]{3,2,1,0:T(1,128)} %refs_4_.1, f32[1,1,1,6]{3,2,1,0:T(1,128)} %refs_5_.1, s32[1,1,1,2]{3,2,1,0:T(1,128)} %refs_6_.1, ...), custom_call_target="tpu_custom_call" | custom-call | tf_op jit(solution)/shard_map/pallas_call | solution.py:597
  34.4 0.9 %copy.12 = f32[1,5,16,2304]{3,2,1,0:T(8,128)} copy(f32[1,5,16,2304]{3,2,1,0:T(8,128)S(1)} %shard_map.100) | data formatting | bytes 1474560
